TPU v7x, 32 devices: a whole 2x2x4 slice. The times are simulated.
32 devices in a mesh: freq: 8 (over z, y), blk: 4 (over x, core).
Axes of the slice: x: 2, y: 2, z: 4, core: 2. Of those that a mesh axis runs over, the one named last changes fastest.
Arguments:
- samples: int32 [1024, 417792], P(('blk', 'freq')), may hold values from -8 to 7
Outputs:
- visibilities: bfloat16 [2, 96, 1024, 1024], P(None, 'freq', 'blk')
All inputs are finite; a program needn't handle non-finite values.
Results may differ from a plain program's by a relative error of at most 0.0079.
Values may be sent and summed in bfloat16 or wider, within the bound.
No kernel may reach another device: no remote copies, remote signals or barrier semaphores. Data moves between devices by JAX's collectives and lax.ppermute only.
A program may use at most 320 MiB of HBM per device.

v0:
```python
import math

import jax
import jax.numpy as jnp
from jax import lax
from jax.sharding import PartitionSpec as P

FRAME = 8192
TAPS = 4
CH_DEV = 12
NSPEC = 48


def make_window(frame, taps):
    length = taps * frame
    moment = jnp.arange(length, dtype=jnp.float32)
    offset = (moment + 0.5 - length / 2.0) / frame
    taper = 0.5 - 0.5 * jnp.cos(2.0 * math.pi * (moment + 0.5) / length)
    return (jnp.sinc(offset) * taper).reshape(taps, frame)


def make_table(frame, channels):
    index = jnp.arange(frame, dtype=jnp.int32)[:, None]
    column = jnp.arange(channels, dtype=jnp.int32)[None, :] + 1
    phase = (index * column % frame).astype(jnp.float32) * (2.0 * math.pi / frame)
    factor = 1.0 / math.sqrt(21.25 * frame)
    both = jnp.concatenate([jnp.cos(phase) * factor, -jnp.sin(phase) * factor], axis=1)
    return both.astype(jnp.bfloat16)


def cross_block(stacked, rotated, right):
    numbers = (((1,), (1,)), ((0,), (0,)))
    real_part = lax.dot_general(stacked, right, numbers, preferred_element_type=jnp.float32)
    imag_part = lax.dot_general(rotated, right, numbers, preferred_element_type=jnp.float32)
    return jnp.stack([real_part, imag_part])


def per_device(samples):
    antennas = samples.shape[0]
    freq_count = lax.axis_size("freq")
    channels = CH_DEV * freq_count
    window = make_window(FRAME, TAPS)
    frames = samples.reshape(antennas, NSPEC + TAPS - 1, FRAME).astype(jnp.float32)
    filtered = frames[:, 0:NSPEC, :] * window[0]
    for k in range(1, TAPS):
        filtered = filtered + frames[:, k : k + NSPEC, :] * window[k]
    filtered = filtered.astype(jnp.bfloat16)
    table = make_table(FRAME, channels).reshape(FRAME, 2, channels)
    spectra = jnp.einsum("fpj,asf->jpsa", table, filtered, preferred_element_type=jnp.float32)
    spectra = spectra.astype(jnp.bfloat16).reshape(channels, 2 * NSPEC, antennas)
    turned = lax.all_to_all(spectra, "freq", split_axis=0, concat_axis=2, tiled=True)
    rotated = jnp.concatenate([turned[:, NSPEC:, :], -turned[:, :NSPEC, :]], axis=1)
    term = cross_block(turned, rotated, lax.all_gather(turned, "blk", axis=2, tiled=True))
    return (term / NSPEC).astype(jnp.bfloat16)


def solution(mesh):
    in_specs = (P(("blk", "freq"), None),)
    out_specs = P(None, "freq", "blk", None)
    return jax.shard_map(
        per_device, mesh=mesh, in_specs=in_specs, out_specs=out_specs, check_vma=False
    )
```

profile of v0, /device:TPU:0, one launch (start us, length us, event | category | flops | bytes accessed | tf_op | source)
XLA Modules:
  0.0 252.4 jit_solution(14777062810074291774)
XLA Ops:
  6.5 0.0 all-gather.2.cloned.1.call-start
  6.5 0.6 fusion.26
  7.2 13.7 %multiply_convert_fusion.1 = (bf16[8192,1,96]{0,2,1:T(8,128)(2,1)S(1)}, bf16[8192,1,96]{0,2,1:T(8,128)(2,1)S(1)}) fusion(s32[96]{0:T(128)S(1)} %iota_add_fusion.2), kind=kLoop, calls=%fused_computation.24 | loop fusion | flops 14942208 | bytes 3146112 | tf_op jit(solution)/shard_map/convert
  20.9 36.6 %convert_element_type.38 = f32[32,417792]{1,0:T(8,128)} convert(s32[32,417792]{1,0:T(8,128)} %param.1) | non-fusion elementwise | flops 13369344 | bytes 106954752 | tf_op jit(solution)/shard_map/convert_element_type | solution.py:43
  57.4 50.3 %convert_element_type.39 = f32[32,51,8192]{2,1,0:T(8,128)} reshape(f32[32,417792]{1,0:T(8,128)} %convert_element_type.38) | data formatting | bytes 106954752 | tf_op jit(solution)/shard_map/convert_element_type | solution.py:43
  107.8 71.7 %fusion.16 = bf16[32,48,2,96]{3,1,2,0:T(8,128)(2,1)} fusion(bf16[8192,1,96]{0,2,1:T(8,128)(2,1)S(1)} %get-tuple-element.12, bf16[8192,1,96]{0,2,1:T(8,128)(2,1)S(1)} %get-tuple-element.11, f32[8192]{0:T(1024)S(1)} %get-tuple-element.8, f32[32,51,8192]{2,1,0:T(8,128)} %convert_element_type.39, f32[8192]{0:T(1024)S(1)} %get-tuple-element.9, ...), kind=kOutput, calls=%fused_computation.28 | convolution fusion | flops 4939087872 | bytes 205193216 | tf_op jit(solution)/shard_map/fpj,asf->jpsa/dot_general | solution.py:49
  179.5 2.2 copy.3
  181.7 27.2 %all_to_all.18 = bf16[96,96,32]{1,2,0:T(8,128)(2,1)S(1)} all-to-all(bf16[96,96,32]{1,2,0:T(8,128)(2,1)S(1)} %copy.3), channel_id=1, replica_groups=mesh['freq'=8,'blk'=4] {'freq'}, dimensions={0} | all-to-all | bytes 1179648 | tf_op jit(solution)/shard_map/all_to_all | solution.py:51
  209.0 0.1 copy.4
  209.0 1.1 copy.5
  210.1 0.0 all-gather.2.cloned.1.call-update
  210.1 1.1 fusion.53
  211.3 22.4 %all-gather.2.cloned.1.call-done = bf16[12,96,1024]{2,1,0:T(8,128)(2,1)} async-done(((bf16[12,96,256]{2,1,0:T(8,128)(2,1)}), bf16[12,96,1024]{2,1,0:T(8,128)(2,1)}) %all-gather.2.cloned.1.call-update) | async-done | bytes 2359312 | tf_op jit(solution)/shard_map/all_gather | solution.py:53
  233.7 0.0 copy-start
  233.7 3.6 %convolution_bitcast_fusion.1 = f32[1,12,256,1024]{3,2,1,0:T(8,128)S(1)} fusion(bf16[12,96,256]{1,2,0:T(8,128)(2,1)S(1)} %bitcast.33, bf16[12,96,1024]{2,1,0:T(8,128)(2,1)} %all-gather.2.cloned.1.call-done), kind=kOutput, calls=%fused_computation.16 | convolution fusion | flops 603979776 | bytes 15532032 | tf_op jit(solution)/shard_map/dot_general | solution.py:33
  237.3 0.0 copy-done
  237.3 1.8 convolution_bitcast_fusion
  239.1 6.5 %fusion.4 = bf16[2,12,256,1024]{3,2,1,0:T(8,128)(2,1)} fusion(f32[1,12,256,1024]{3,2,1,0:T(8,128)S(1)} %convolution_bitcast_fusion, f32[1,12,256,1024]{3,2,1,0:T(8,128)S(1)} %convolution_bitcast_fusion.1), kind=kLoop, calls=%fused_computation.9 | loop fusion | flops 18874368 | bytes 37748736 | tf_op jit(solution)/shard_map/convert_element_type | solution.py:54
  (2 shorter events, 0.0 us)
Async XLA Ops:
  6.5 227.1 %all-gather.2.cloned.1.call-start = ((), (), s32[]{:S(2)}) async-start(), calls=%async_computation.1 | async-start | bytes 2949120 | tf_op jit(solution)/shard_map/all_gather | solution.py:53
  233.7 3.6 %copy-start = (bf16[12,96,1024]{2,1,0:T(8,128)(2,1)S(1)}, bf16[12,96,1024]{2,1,0:T(8,128)(2,1)}, u32[]{:S(2)}) copy-start(bf16[12,96,1024]{2,1,0:T(8,128)(2,1)} %all-gather.2.cloned.1.call-done) | copy-start | bytes 7077892
Sparse Core Ops, SparseCore 0:
  210.3 23.3 all-gather.1
where the time goes:
time: 253 us; the launch traced here: 252 us
  matrix products  77.2 us (31%)
  other arithmetic  58.5 us (23%)
  local copies, waits for them, and re-layouts  53.7 us (21%)
  blocking collectives  27.2 us (11%)
  waiting for transfers between devices  22.4 us (9%)
  between operations  13.4 us (5%)
    dot_general x1, matrix products, per_device(): jnp.einsum('fpj,asf->jpsa', table, filtered, preferred_element_type=jnp.f...  71.7 us
    convert_element_type x1, local copies, waits for them, and re-layouts, per_device(): samples.reshape(antennas, NSPEC + TAPS - 1, FRAME).astype(jnp.float32)  50.3 us
    convert_element_type x1, other arithmetic, per_device(): samples.reshape(antennas, NSPEC + TAPS - 1, FRAME).astype(jnp.float32)  36.6 us
    all_to_all x1, blocking collectives, per_device(): lax.all_to_all(spectra, 'freq', split_axis=0, concat_axis=2, tiled=True)  27.2 us
    all_gather x1, waiting for transfers between devices, per_device(): lax.all_gather(turned, 'blk', axis=2, tiled=True)  22.4 us
    another operation x1, other arithmetic  13.7 us
    convert_element_type x1, other arithmetic, per_device(): return (term / NSPEC).astype(jnp.bfloat16)  6.49 us
  transfers between devices with their start and end apart: 1, of which 1 were waited for; matrix products, arithmetic and copies ran while one was open for 0% of the time, Pallas kernels for 0%

commit v1 on v0

v1 whole, which is shorter than its diff:
```python
import math

import jax
import jax.numpy as jnp
import ml_dtypes
import numpy as np
from jax import lax
from jax.experimental import pallas as pl
from jax.experimental.pallas import tpu as pltpu
from jax.sharding import PartitionSpec as P

FRAME = 8192
TAPS = 4
CH_DEV = 12
NSPEC = 48
LANES = 128
PAIR = 2 * NSPEC
BLOCK = 1024
VMEM_LIMIT = 48 * 1024 * 1024


def make_window(frame, taps):
    length = taps * frame
    moment = np.arange(length, dtype=np.float64)
    offset = (moment + 0.5 - length / 2.0) / frame
    taper = 0.5 - 0.5 * np.cos(2.0 * math.pi * (moment + 0.5) / length)
    return (np.sinc(offset) * taper).astype(np.float32).reshape(taps, frame)


def make_table(frame, channels, width):
    index = np.arange(frame, dtype=np.int64)[:, None]
    column = np.arange(channels, dtype=np.int64)[None, :] + 1
    phase = (index * column % frame).astype(np.float64) * (2.0 * math.pi / frame)
    factor = 1.0 / math.sqrt(21.25 * frame)
    table = np.zeros((frame, 2 * width), np.float32)
    table[:, :channels] = np.cos(phase) * factor
    table[:, width : width + channels] = -np.sin(phase) * factor
    return table.astype(ml_dtypes.bfloat16)


def filterbank_kernel(rows, channels, width, x_ref, w_ref, t_ref, o_ref, filt, acc, turned):
    step = pl.program_id(0)
    groups = rows // 8
    tiles = BLOCK // LANES

    def one_tile(tile, carry):
        lanes = pl.ds(pl.multiple_of(tile * LANES, LANES), LANES)
        taps = [w_ref[pl.ds(k, 1), lanes] for k in range(TAPS)]
        held = [[x_ref[g, f, tile].astype(jnp.float32) for f in range(TAPS - 1)] for g in range(groups)]
        pending = []
        for s in range(NSPEC):
            for g in range(groups):
                held[g].append(x_ref[g, s + TAPS - 1, tile].astype(jnp.float32))
                total = held[g][0] * taps[0]
                for k in range(1, TAPS):
                    total = total + held[g][k] * taps[k]
                held[g].pop(0)
                pending.append(total)
                if len(pending) == 2:
                    row = (s * groups + g - 1) * 8
                    filt[pl.ds(row, 16), lanes] = jnp.concatenate(pending, axis=0).astype(jnp.bfloat16)
                    pending = []
        return carry

    lax.fori_loop(0, tiles, one_tile, 0)
    part = jnp.dot(filt[...], t_ref[...], preferred_element_type=jnp.float32)

    halves = [part[:, h * LANES : (h + 1) * LANES] for h in range(2 * width // LANES)]

    @pl.when(step == 0)
    def _():
        for h, half in enumerate(halves):
            acc[h] = half

    @pl.when(step > 0)
    def _():
        for h, half in enumerate(halves):
            acc[h] += half

    @pl.when(step == pl.num_programs(0) - 1)
    def _():
        for c in range(width // LANES):
            count = min(LANES, channels - c * LANES)
            for a in range(rows):
                both = jnp.concatenate(
                    [
                        acc[p * (width // LANES) + c, pl.ds(a, NSPEC, stride=rows), :]
                        for p in range(2)
                    ],
                    axis=0,
                )
                turned[pl.ds(c * LANES * rows + a, count, stride=rows), pl.ds(0, PAIR)] = both.T[:count]
        lane = lax.broadcasted_iota(jnp.int32, (rows, LANES), 1)
        for q in range(channels // 4):
            one = [turned[pl.ds((4 * q + i) * rows, rows), :] for i in range(4)]
            one = [one[0]] + [pltpu.roll(one[i], LANES - 32 * i, 1) for i in range(1, 4)]
            out = [jnp.where(lane < LANES - 32 * (i + 1), one[i], one[i + 1]) for i in range(3)]
            out = jnp.concatenate(out, axis=1).astype(jnp.bfloat16)
            dest, place = q // (CH_DEV // 4), q % (CH_DEV // 4)
            o_ref[dest, :, pl.ds(place * 384, 384)] = out


def filterbank(samples, window, table, piece, rows, shards):
    antenna_groups, frames, steps, _, _ = samples.shape
    groups = rows // 8
    channels = CH_DEV * shards
    width = table.shape[1] // 2
    tiles = BLOCK // LANES
    spec_rows = NSPEC * rows
    flops = 2 * spec_rows * FRAME * 2 * width
    return pl.pallas_call(
        lambda *refs: filterbank_kernel(rows, channels, width, *refs),
        grid=(FRAME // BLOCK,),
        in_specs=[
            pl.BlockSpec((groups, frames, tiles, 8, LANES), lambda i: (piece, 0, i, 0, 0)),
            pl.BlockSpec((TAPS, BLOCK), lambda i: (0, i)),
            pl.BlockSpec((BLOCK, 2 * width), lambda i: (i, 0)),
        ],
        out_specs=pl.BlockSpec((shards, rows, CH_DEV * PAIR), lambda i: (0, 0, 0)),
        out_shape=jax.ShapeDtypeStruct((shards, rows, CH_DEV * PAIR), jnp.bfloat16),
        scratch_shapes=[
            pltpu.VMEM((spec_rows, BLOCK), jnp.bfloat16),
            pltpu.VMEM((2 * width // LANES, spec_rows, LANES), jnp.float32),
            pltpu.VMEM((channels * rows, LANES), jnp.float32),
        ],
        compiler_params=pltpu.CompilerParams(vmem_limit_bytes=VMEM_LIMIT),
        cost_estimate=pl.CostEstimate(
            flops=flops, bytes_accessed=4 * rows * frames * FRAME, transcendentals=0
        ),
        name="filterbank",
    )(samples, window, table)


def correlate_kernel(pieces, rows, shards, blocks, *refs):
    place, own = refs[0], refs[1 : 1 + pieces]
    cols = refs[1 + pieces : 1 + pieces + blocks * pieces]
    out = refs[-1]
    step = pl.program_id(0)
    local = shards * pieces * rows
    base = pl.multiple_of((step // 2) * 384 + (step % 2) * LANES, LANES)
    window = pl.ds(base, 256)

    def gather(parts):
        loaded = [part[:, :, window] for part in parts]
        return jnp.stack(loaded, axis=1).reshape(local, 256)

    mine = gather(own).astype(jnp.float32)
    lane = lax.broadcasted_iota(jnp.int32, (local, 256), 1)
    ahead, behind = pltpu.roll(mine, 256 - NSPEC, 1), pltpu.roll(mine, NSPEC, 1)
    left = []
    for i in range(2):
        start = lane - ((step % 2) * 64 + i * PAIR)
        real = (start >= 0) & (start < NSPEC)
        imag = (start >= NSPEC) & (start < PAIR)
        left.append(jnp.where(real | imag, mine, 0.0).astype(jnp.bfloat16))
        left.append(jnp.where(real, ahead, jnp.where(imag, -behind, 0.0)).astype(jnp.bfloat16))
    left = jnp.concatenate(left, axis=0)
    for n in range(blocks):
        right = gather(cols[n * pieces : (n + 1) * pieces])
        term = lax.dot_general(left, right, (((1,), (1,)), ((), ())), preferred_element_type=jnp.float32)
        term = (term * (1.0 / NSPEC)).astype(jnp.bfloat16)
        at = pl.ds(pl.multiple_of(place[n] * local, LANES), local)
        for i in range(2):
            for p in range(2):
                k = 2 * i + p
                out[p, i, :, at] = term[k * local : (k + 1) * local]


def correlate(place, own, cols, width):
    pieces = len(own)
    blocks = len(cols) // pieces
    shards, rows, depth = own[0].shape
    local = shards * pieces * rows
    whole = pl.BlockSpec((shards, rows, depth), lambda i, *_: (0, 0, 0))
    return pl.pallas_call(
        lambda *refs: correlate_kernel(pieces, rows, shards, blocks, *refs),
        grid_spec=pltpu.PrefetchScalarGridSpec(
            num_scalar_prefetch=1,
            grid=(CH_DEV // 2,),
            in_specs=[whole] * (pieces + len(cols)),
            out_specs=pl.BlockSpec((2, 2, local, width), lambda i, *_: (0, i, 0, 0)),
        ),
        out_shape=jax.ShapeDtypeStruct((2, CH_DEV, local, width), jnp.bfloat16),
        compiler_params=pltpu.CompilerParams(vmem_limit_bytes=VMEM_LIMIT),
        cost_estimate=pl.CostEstimate(
            flops=2 * 2 * CH_DEV * local * local * blocks * 256,
            bytes_accessed=2 * 2 * CH_DEV * local * local * blocks,
            transcendentals=0,
        ),
        name="correlate",
    )(place, *own, *cols)


def exchange(value, axis, distance):
    count = lax.axis_size(axis)
    return lax.ppermute(value, axis, [(i, i ^ distance) for i in range(count)])


def per_device(samples):
    antennas, length = samples.shape
    shards = lax.axis_size("freq")
    blocks = lax.axis_size("blk")
    channels = CH_DEV * shards
    frames = length // FRAME
    width = -(-channels // LANES) * LANES
    rows = 16 if antennas % 16 == 0 else 8
    pieces = antennas // rows
    window = jnp.asarray(make_window(FRAME, TAPS))
    table = jnp.asarray(make_table(FRAME, channels, width))
    tiled = samples.reshape(antennas // 8, 8, length // LANES, LANES).transpose(0, 2, 1, 3)
    tiled = tiled.reshape(antennas // 8, frames, FRAME // LANES, 8, LANES)
    held = []
    for piece in range(pieces):
        spectra = filterbank(tiled, window, table, piece, rows, shards)
        turned = lax.all_to_all(spectra, "freq", split_axis=0, concat_axis=0, tiled=True)
        far = exchange(turned, "blk", 2)
        near = exchange(turned, "blk", 1)
        last = exchange(far, "blk", 1)
        held.append([turned, near, far, last])
    me = lax.axis_index("blk")
    place = jnp.stack([me ^ n for n in range(blocks)]).astype(jnp.int32)
    own = [held[p][0] for p in range(pieces)]
    cols = [held[p][n] for n in range(blocks) for p in range(pieces)]
    return correlate(place, own, cols, antennas * shards * blocks)


def solution(mesh):
    in_specs = (P(("blk", "freq"), None),)
    out_specs = P(None, "freq", "blk", None)
    return jax.shard_map(
        per_device, mesh=mesh, in_specs=in_specs, out_specs=out_specs, check_vma=False
    )
```

time: 253 us -> 79.9 us (0.32)
  matrix products: 77.2 us -> 0 us
  other arithmetic: 58.5 us -> 0.08 us
  local copies, waits for them, and re-layouts: 53.7 us -> 5.28 us
  Pallas kernels: 0 us -> 43.2 us
  blocking collectives: 27.2 us -> 0 us
  starting transfers between devices: 0.01 us -> 16.8 us
  between operations: 13.4 us -> 0.03 us
  waiting for transfers between devices: 22.4 us -> 13.7 us
    dot_general x3 -> x0, matrix products: 77.2 us -> none  [the longest x1 71.7 us: per_device(): jnp.einsum('fpj,asf->jpsa', table, filtered, preferred_element_type=jnp.f...]
    convert_element_type x1 -> x0, local copies, waits for them, and re-layouts: 50.3 us -> none  [per_device(): samples.reshape(antennas, NSPEC + TAPS - 1, FRAME).astype(jnp.float32)]
    pallas_call x0 -> x3, Pallas kernels: none -> 43.2 us  [the longest x2 35 us: filterbank(): pl.pallas_call(lambda *refs: filterbank_kernel(rows, channels, width, *re...]
    convert_element_type x2 -> x0, other arithmetic: 43.1 us -> none  [the longest x1 36.6 us: per_device(): samples.reshape(antennas, NSPEC + TAPS - 1, FRAME).astype(jnp.float32)]
    all_to_all x1 -> x0, blocking collectives: 27.2 us -> none  [per_device(): lax.all_to_all(spectra, 'freq', split_axis=0, concat_axis=2, tiled=True)]
    all_gather x1 -> x0, waiting for transfers between devices: 22.4 us -> none  [per_device(): lax.all_gather(turned, 'blk', axis=2, tiled=True)]
    another operation x1, other arithmetic: 13.7 us -> 0.08 us  [per_device(): place = jnp.stack([me ^ n for n in range(blocks)]).astype(jnp.int32)]
    all_to_all x0 -> x2, starting transfers between devices: none -> 13.3 us  [per_device(): lax.all_to_all(spectra, 'freq', split_axis=0, concat_axis=0, tiled=True)]
  transfers between devices with their start and end apart: 1 -> 8, of which waited for: 1 -> 3; matrix products, arithmetic and copies ran while one was open for 0% -> 0% of each run, Pallas kernels for 0% -> 22%
where the time goes in v1:
time: 79.9 us; the launch traced here: 79.1 us
  Pallas kernels  43.2 us (54%)
  starting transfers between devices  16.8 us (21%)
  waiting for transfers between devices  13.7 us (17%)
  local copies, waits for them, and re-layouts  5.28 us (7%)
    pallas_call x2, Pallas kernels, filterbank(): pl.pallas_call(lambda *refs: filterbank_kernel(rows, channels, width, *re...  35 us
    all_to_all x2, starting transfers between devices, per_device(): lax.all_to_all(spectra, 'freq', split_axis=0, concat_axis=0, tiled=True)  13.3 us
    pallas_call x1, Pallas kernels, correlate(): pl.pallas_call(lambda *refs: correlate_kernel(pieces, rows, shards, block...  8.28 us
    all_to_all x2, waiting for transfers between devices, per_device(): lax.all_to_all(spectra, 'freq', split_axis=0, concat_axis=0, tiled=True)  7.53 us
    ppermute x6, waiting for transfers between devices, exchange(): return lax.ppermute(value, axis, [(i, i ^ distance) for i in range(count)])  6.21 us
    unnamed x8, local copies, waits for them, and re-layouts  5.28 us
    ppermute x6, starting transfers between devices, exchange(): return lax.ppermute(value, axis, [(i, i ^ distance) for i in range(count)])  3.5 us
  transfers between devices with their start and end apart: 8, of which 3 were waited for; matrix products, arithmetic and copies ran while one was open for 0% of the time, Pallas kernels for 22%

profile of v1, /device:TPU:0, one launch (start us, length us, event | category | flops | bytes accessed | tf_op | source)
XLA Modules:
  0.0 79.1 jit_solution(8113673613796152860)
XLA Ops:
  0.0 0.0 copy-start
  0.0 2.2 %copy-done = bf16[8192,256]{1,0:T(8,128)(2,1)S(1)} copy-done((bf16[8192,256]{1,0:T(8,128)(2,1)S(1)}, bf16[8192,256]{1,0:T(8,128)(2,1)}, u32[]{:S(2)}) %copy-start) | copy-done | bytes 4194328
  2.2 0.0 copy-start.2
  2.2 0.9 %copy-done.2 = f32[4,8192]{1,0:T(4,128)S(1)} copy-done((f32[4,8192]{1,0:T(4,128)S(1)}, f32[4,8192]{1,0:T(4,128)}, u32[]{:S(2)}) %copy-start.2) | copy-done | bytes 131096
  3.1 0.0 copy-start.3
  3.1 17.5 %filterbank.2 = bf16[8,16,1152]{2,1,0:T(8,128)(2,1)} custom-call(s32[4,51,64,8,128]{4,3,2,1,0:T(8,128)} %bitcast.9, f32[4,8192]{1,0:T(4,128)S(1)} %copy-done.2, bf16[8192,256]{1,0:T(8,128)(2,1)S(1)} %copy-done), custom_call_target="tpu_custom_call" | custom-call | flops 3221225472 | bytes 26738688 | tf_op jit(solution)/shard_map/filterbank/pallas_call | solution.py:111
  20.6 7.3 %all-to-all-start = ((bf16[8,16,1152]{2,1,0:T(8,128)(2,1)}), bf16[8,16,1152]{2,1,0:T(8,128)(2,1)S(1)}, u32[]{:S(2)}, u32[]{:S(2)}) async-start(bf16[8,16,1152]{2,1,0:T(8,128)(2,1)} %filterbank.2), calls=%async_computation | async-start | bytes 589824 | tf_op jit(solution)/shard_map/all_to_all | solution.py:215
  27.9 0.0 copy-done.3
  27.9 0.0 copy-start.1
  27.9 2.2 %copy-done.1 = bf16[8192,256]{1,0:T(8,128)(2,1)S(1)} copy-done((bf16[8192,256]{1,0:T(8,128)(2,1)S(1)}, bf16[8192,256]{1,0:T(8,128)(2,1)}, u32[]{:S(2)}) %copy-start.1) | copy-done | bytes 4194328
  30.1 17.5 %filterbank.3 = bf16[8,16,1152]{2,1,0:T(8,128)(2,1)} custom-call(s32[4,51,64,8,128]{4,3,2,1,0:T(8,128)} %bitcast.10, f32[4,8192]{1,0:T(4,128)S(1)} %copy-done.3, bf16[8192,256]{1,0:T(8,128)(2,1)S(1)} %copy-done.1), custom_call_target="tpu_custom_call" | custom-call | flops 3221225472 | bytes 26738688 | tf_op jit(solution)/shard_map/filterbank/pallas_call | solution.py:111
  47.5 0.0 all-to-all-done.refs_1_.refs_3_
  47.5 6.0 %all-to-all-start.1 = ((bf16[8,16,1152]{2,1,0:T(8,128)(2,1)}), bf16[8,16,1152]{2,1,0:T(8,128)(2,1)S(1)}, u32[]{:S(2)}, u32[]{:S(2)}) async-start(bf16[8,16,1152]{2,1,0:T(8,128)(2,1)} %filterbank.3), calls=%async_computation.1 | async-start | bytes 589824 | tf_op jit(solution)/shard_map/all_to_all | solution.py:215
  53.5 1.5 %collective-permute-start.2 = (bf16[8,16,1152]{2,1,0:T(8,128)(2,1)S(1)}, bf16[8,16,1152]{2,1,0:T(8,128)(2,1)S(1)}, u32[]{:S(2)}, u32[]{:S(2)}) collective-permute-start(bf16[8,16,1152]{2,1,0:T(8,128)(2,1)S(1)} %all-to-all-done.refs_1_.refs_3_), channel_id=1, source_target_pairs={{0,2},{1,3},{2,0},{3,1},{4,6},{5,7},{6,4},{7,5},{8,10},{9,11},{10,... | collective-permute-start | bytes 884744 | tf_op jit(solution)/shard_map/ppermute | solution.py:196
  55.0 7.5 %all-to-all-done.1.refs_2_.refs_4_ = bf16[8,16,1152]{2,1,0:T(8,128)(2,1)S(1)} async-done(((bf16[8,16,1152]{2,1,0:T(8,128)(2,1)}), bf16[8,16,1152]{2,1,0:T(8,128)(2,1)S(1)}, u32[]{:S(2)}, u32[]{:S(2)}) %all-to-all-start.1) | async-done | bytes 294944 | tf_op jit(solution)/shard_map/all_to_all | solution.py:215
  62.5 1.5 %collective-permute-start.3 = (bf16[8,16,1152]{2,1,0:T(8,128)(2,1)S(1)}, bf16[8,16,1152]{2,1,0:T(8,128)(2,1)S(1)}, u32[]{:S(2)}, u32[]{:S(2)}) collective-permute-start(bf16[8,16,1152]{2,1,0:T(8,128)(2,1)S(1)} %all-to-all-done.1.refs_2_.refs_4_), channel_id=1, source_target_pairs={{0,2},{1,3},{2,0},{3,1},{4,6},{5,7},{6,4},{7,5},{8,10},{9,11},{10,... | collective-permute-start | bytes 884744 | tf_op jit(solution)/shard_map/ppermute | solution.py:196
  64.0 0.0 collective-permute-start
  64.0 0.5 collective-permute-start.1
  64.5 0.0 collective-permute-done.2.refs_7_
  64.5 0.0 collective-permute-start.4
  64.6 4.7 %collective-permute-done.3.refs_8_ = bf16[8,16,1152]{2,1,0:T(8,128)(2,1)S(1)} collective-permute-done((bf16[8,16,1152]{2,1,0:T(8,128)(2,1)S(1)}, bf16[8,16,1152]{2,1,0:T(8,128)(2,1)S(1)}, u32[]{:S(2)}, u32[]{:S(2)}) %collective-permute-start.3) | collective-permute-done | bytes 294944 | tf_op jit(solution)/shard_map/ppermute | solution.py:196
  69.3 0.0 collective-permute-start.5
  69.3 0.1 pad_add_fusion.refs_0_
  69.3 0.0 collective-permute-done.refs_5_
  69.3 0.0 collective-permute-done.1.refs_6_
  69.4 0.0 collective-permute-done.4.refs_9_
  69.4 1.5 %collective-permute-done.5.refs_10_ = bf16[8,16,1152]{2,1,0:T(8,128)(2,1)S(1)} collective-permute-done((bf16[8,16,1152]{2,1,0:T(8,128)(2,1)S(1)}, bf16[8,16,1152]{2,1,0:T(8,128)(2,1)S(1)}, u32[]{:S(2)}, u32[]{:S(2)}) %collective-permute-start.5) | collective-permute-done | bytes 294944 | tf_op jit(solution)/shard_map/ppermute | solution.py:196
  70.8 8.3 %correlate.1 = bf16[2,12,256,1024]{3,2,1,0:T(8,128)(2,1)} custom-call(s32[4]{0:T(128)S(1)} %pad_add_fusion.refs_0_, bf16[8,16,1152]{2,1,0:T(8,128)(2,1)S(1)} %all-to-all-done.refs_1_.refs_3_, bf16[8,16,1152]{2,1,0:T(8,128)(2,1)S(1)} %all-to-all-done.1.refs_2_.refs_4_, bf16[8,16,1152]{2,1,0:T(8,128)(2,1)S(1)} %all-to-all-done.refs_1_.refs_3_, ...), custom_call_target="tpu_custom_call" | custom-call | flops 3221225472 | bytes 12582912 | tf_op jit(solution)/shard_map/correlate/pallas_call | solution.py:175
Async XLA Ops:
  0.0 2.2 %copy-start = (bf16[8192,256]{1,0:T(8,128)(2,1)S(1)}, bf16[8192,256]{1,0:T(8,128)(2,1)}, u32[]{:S(2)}) copy-start(bf16[8192,256]{1,0:T(8,128)(2,1)} %constant.15.clone.refs_2_) | copy-start | bytes 12582916
  2.2 0.9 %copy-start.2 = (f32[4,8192]{1,0:T(4,128)S(1)}, f32[4,8192]{1,0:T(4,128)}, u32[]{:S(2)}) copy-start(f32[4,8192]{1,0:T(4,128)} %constant.14.clone.refs_1_) | copy-start | bytes 393220
  3.1 24.8 %copy-start.3 = (f32[4,8192]{1,0:T(4,128)S(1)}, f32[4,8192]{1,0:T(4,128)}, u32[]{:S(2)}) copy-start(f32[4,8192]{1,0:T(4,128)} %constant.14.clone.refs_1_) | copy-start | bytes 393220
  20.6 26.9 %all-to-all-start = ((bf16[8,16,1152]{2,1,0:T(8,128)(2,1)}), bf16[8,16,1152]{2,1,0:T(8,128)(2,1)S(1)}, u32[]{:S(2)}, u32[]{:S(2)}) async-start(bf16[8,16,1152]{2,1,0:T(8,128)(2,1)} %filterbank.2), calls=%async_computation | async-start | bytes 589824 | tf_op jit(solution)/shard_map/all_to_all | solution.py:215
  27.9 2.2 %copy-start.1 = (bf16[8192,256]{1,0:T(8,128)(2,1)S(1)}, bf16[8192,256]{1,0:T(8,128)(2,1)}, u32[]{:S(2)}) copy-start(bf16[8192,256]{1,0:T(8,128)(2,1)} %constant.15.clone.refs_2_) | copy-start | bytes 12582916
  47.5 15.0 %all-to-all-start.1 = ((bf16[8,16,1152]{2,1,0:T(8,128)(2,1)}), bf16[8,16,1152]{2,1,0:T(8,128)(2,1)S(1)}, u32[]{:S(2)}, u32[]{:S(2)}) async-start(bf16[8,16,1152]{2,1,0:T(8,128)(2,1)} %filterbank.3), calls=%async_computation.1 | async-start | bytes 589824 | tf_op jit(solution)/shard_map/all_to_all | solution.py:215
  53.5 11.0 %collective-permute-start.2 = (bf16[8,16,1152]{2,1,0:T(8,128)(2,1)S(1)}, bf16[8,16,1152]{2,1,0:T(8,128)(2,1)S(1)}, u32[]{:S(2)}, u32[]{:S(2)}) collective-permute-start(bf16[8,16,1152]{2,1,0:T(8,128)(2,1)S(1)} %all-to-all-done.refs_1_.refs_3_), channel_id=1, source_target_pairs={{0,2},{1,3},{2,0},{3,1},{4,6},{5,7},{6,4},{7,5},{8,10},{9,11},{10,... | collective-permute-start | bytes 884744 | tf_op jit(solution)/shard_map/ppermute | solution.py:196
  62.5 6.7 %collective-permute-start.3 = (bf16[8,16,1152]{2,1,0:T(8,128)(2,1)S(1)}, bf16[8,16,1152]{2,1,0:T(8,128)(2,1)S(1)}, u32[]{:S(2)}, u32[]{:S(2)}) collective-permute-start(bf16[8,16,1152]{2,1,0:T(8,128)(2,1)S(1)} %all-to-all-done.1.refs_2_.refs_4_), channel_id=1, source_target_pairs={{0,2},{1,3},{2,0},{3,1},{4,6},{5,7},{6,4},{7,5},{8,10},{9,11},{10,... | collective-permute-start | bytes 884744 | tf_op jit(solution)/shard_map/ppermute | solution.py:196
  64.0 5.3 %collective-permute-start = (bf16[8,16,1152]{2,1,0:T(8,128)(2,1)S(1)}, bf16[8,16,1152]{2,1,0:T(8,128)(2,1)S(1)}, u32[]{:S(2)}, u32[]{:S(2)}) collective-permute-start(bf16[8,16,1152]{2,1,0:T(8,128)(2,1)S(1)} %all-to-all-done.refs_1_.refs_3_), channel_id=1, source_target_pairs={{0,1},{1,0},{2,3},{3,2},{4,5},{5,4},{6,7},{7,6},{8,9},{9,8},{10,11... | collective-permute-start | bytes 884744 | tf_op jit(solution)/shard_map/ppermute | solution.py:196
  64.0 5.3 %collective-permute-start.1 = (bf16[8,16,1152]{2,1,0:T(8,128)(2,1)S(1)}, bf16[8,16,1152]{2,1,0:T(8,128)(2,1)S(1)}, u32[]{:S(2)}, u32[]{:S(2)}) collective-permute-start(bf16[8,16,1152]{2,1,0:T(8,128)(2,1)S(1)} %all-to-all-done.1.refs_2_.refs_4_), channel_id=1, source_target_pairs={{0,1},{1,0},{2,3},{3,2},{4,5},{5,4},{6,7},{7,6},{8,9},{9,8},{10,11... | collective-permute-start | bytes 884744 | tf_op jit(solution)/shard_map/ppermute | solution.py:196
  64.5 4.8 %collective-permute-start.4 = (bf16[8,16,1152]{2,1,0:T(8,128)(2,1)S(1)}, bf16[8,16,1152]{2,1,0:T(8,128)(2,1)S(1)}, u32[]{:S(2)}, u32[]{:S(2)}) collective-permute-start(bf16[8,16,1152]{2,1,0:T(8,128)(2,1)S(1)} %collective-permute-done.2.refs_7_), channel_id=1, source_target_pairs={{0,1},{1,0},{2,3},{3,2},{4,5},{5,4},{6,7},{7,6},{8,9},{9,8},{10,11... | collective-permute-start | bytes 884744 | tf_op jit(solution)/shard_map/ppermute | solution.py:196
  69.3 1.6 %collective-permute-start.5 = (bf16[8,16,1152]{2,1,0:T(8,128)(2,1)S(1)}, bf16[8,16,1152]{2,1,0:T(8,128)(2,1)S(1)}, u32[]{:S(2)}, u32[]{:S(2)}) collective-permute-start(bf16[8,16,1152]{2,1,0:T(8,128)(2,1)S(1)} %collective-permute-done.3.refs_8_), channel_id=1, source_target_pairs={{0,1},{1,0},{2,3},{3,2},{4,5},{5,4},{6,7},{7,6},{8,9},{9,8},{10,11... | collective-permute-start | bytes 884744 | tf_op jit(solution)/shard_map/ppermute | solution.py:196

commit v2 on v1

v2 whole, which is shorter than its diff:
```python
import math

import jax
import jax.numpy as jnp
import ml_dtypes
import numpy as np
from jax import lax
from jax.experimental import pallas as pl
from jax.experimental.pallas import tpu as pltpu
from jax.sharding import PartitionSpec as P

FRAME = 8192
TAPS = 4
CH_DEV = 12
NSPEC = 48
LANES = 128
PAIR = 2 * NSPEC
BLOCK = 2048
PARTS = ((0, 4), (4, 4), (8, 8), (16, 16), (32, 16), (48, 16))
FILTER_VMEM = 60 * 1024 * 1024
CORRELATE_VMEM = 32 * 1024 * 1024


def make_window(frame, taps):
    length = taps * frame
    moment = np.arange(length, dtype=np.float64)
    offset = (moment + 0.5 - length / 2.0) / frame
    taper = 0.5 - 0.5 * np.cos(2.0 * math.pi * (moment + 0.5) / length)
    return (np.sinc(offset) * taper).astype(np.float32).reshape(taps, frame)


def make_table(frame, channels, width):
    index = np.arange(frame, dtype=np.int64)[:, None]
    column = np.arange(channels, dtype=np.int64)[None, :] + 1
    phase = (index * column % frame).astype(np.float64) * (2.0 * math.pi / frame)
    factor = 1.0 / math.sqrt(21.25 * frame)
    table = np.zeros((frame, 2 * width), np.float32)
    table[:, :channels] = np.cos(phase) * factor
    table[:, width : width + channels] = -np.sin(phase) * factor
    return table.astype(ml_dtypes.bfloat16)


def filterbank_kernel(piece, rows, channels, width, x_hbm, w_ref, t_hbm, o_ref, x_ref, t_ref, filt, acc, turned, x_sem, t_sem):
    groups = rows // 8
    spec_rows = NSPEC * rows
    tiles = BLOCK // LANES

    def x_copy(n):
        first, count = PARTS[n]
        where = pl.ds(first, count)
        return pltpu.make_async_copy(
            x_hbm.at[pl.ds(piece * groups, groups), :, where], x_ref.at[:, :, where], x_sem.at[n]
        )

    def t_copy(b):
        return pltpu.make_async_copy(t_hbm.at[pl.ds(b * BLOCK, BLOCK)], t_ref.at[b], t_sem.at[b])

    for n, (first, count) in enumerate(PARTS):
        x_copy(n).start()
        if (first + count) % tiles == 0:
            t_copy(first // tiles).start()

    def one_tile(tile, slot):
        taps = [w_ref[pl.ds(k, 1), pl.ds(pl.multiple_of(tile * LANES, LANES), LANES)] for k in range(TAPS)]
        held = [[x_ref[g, f, tile].astype(jnp.float32) for f in range(TAPS - 1)] for g in range(groups)]
        ready = []
        for s in range(NSPEC):
            for g in range(groups):
                held[g].append(x_ref[g, s + TAPS - 1, tile].astype(jnp.float32))
                total = held[g][0] * taps[0]
                for k in range(1, TAPS):
                    total = total + held[g][k] * taps[k]
                held[g].pop(0)
                ready.append(total)
                if len(ready) == 2:
                    row = (s * groups + g - 1) * 8
                    filt[slot, pl.ds(row, 16), :] = jnp.concatenate(ready, axis=0).astype(jnp.bfloat16)
                    ready = []

    for n, (first, count) in enumerate(PARTS):
        x_copy(n).wait()
        base = first % tiles

        def step(i, carry, first=first, base=base):
            one_tile(first + i, base + i)
            return carry

        lax.fori_loop(0, count, step, 0)
        if (first + count) % tiles:
            continue
        b = first // tiles
        t_copy(b).wait()
        left = jnp.concatenate([filt[k] for k in range(tiles)], axis=1)
        for m in range(2):
            span = slice(m * spec_rows // 2, (m + 1) * spec_rows // 2)
            part = jnp.dot(left[span], t_ref[b], preferred_element_type=jnp.float32)
            for h in range(2 * width // LANES):
                half = part[:, h * LANES : (h + 1) * LANES]
                if b == 0:
                    acc[h, span] = half
                else:
                    acc[h, span] += half

    for c in range(width // LANES):
        count = min(LANES, channels - c * LANES)
        for a in range(rows):
            both = jnp.concatenate(
                [acc[p * (width // LANES) + c, pl.ds(a, NSPEC, stride=rows), :] for p in range(2)], axis=0
            )
            turned[pl.ds(c * LANES * rows + a, count, stride=rows), pl.ds(0, PAIR)] = both.T[:count]
    lane = lax.broadcasted_iota(jnp.int32, (rows, LANES), 1)
    for q in range(channels // 4):
        one = [turned[pl.ds((4 * q + i) * rows, rows), :] for i in range(4)]
        one = [one[0]] + [pltpu.roll(one[i], LANES - 32 * i, 1) for i in range(1, 4)]
        dest, place = q // (CH_DEV // 4), q % (CH_DEV // 4)
        for i in range(3):
            tile = jnp.where(lane < LANES - 32 * (i + 1), one[i], one[i + 1])
            o_ref[dest, place * 3 + i] = tile.astype(jnp.bfloat16)


def filterbank(samples, window, table, piece, rows, shards):
    antenna_groups, frames, _, _, _ = samples.shape
    groups = rows // 8
    channels = CH_DEV * shards
    width = table.shape[1] // 2
    spec_rows = NSPEC * rows
    shape = (shards, CH_DEV * PAIR // LANES, rows, LANES)
    return pl.pallas_call(
        lambda *refs: filterbank_kernel(piece, rows, channels, width, *refs),
        in_specs=[
            pl.BlockSpec(memory_space=pl.ANY),
            pl.BlockSpec(memory_space=pltpu.VMEM),
            pl.BlockSpec(memory_space=pl.ANY),
        ],
        out_specs=pl.BlockSpec(memory_space=pltpu.VMEM),
        out_shape=jax.ShapeDtypeStruct(shape, jnp.bfloat16),
        scratch_shapes=[
            pltpu.VMEM((groups, frames, FRAME // LANES, 8, LANES), jnp.int32),
            pltpu.VMEM((FRAME // BLOCK, BLOCK, 2 * width), jnp.bfloat16),
            pltpu.VMEM((BLOCK // LANES, spec_rows, LANES), jnp.bfloat16),
            pltpu.VMEM((2 * width // LANES, spec_rows, LANES), jnp.float32),
            pltpu.VMEM((channels * rows, LANES), jnp.float32),
            pltpu.SemaphoreType.DMA((len(PARTS),)),
            pltpu.SemaphoreType.DMA((FRAME // BLOCK,)),
        ],
        compiler_params=pltpu.CompilerParams(vmem_limit_bytes=FILTER_VMEM),
        cost_estimate=pl.CostEstimate(
            flops=2 * spec_rows * FRAME * 2 * width, bytes_accessed=4 * rows * frames * FRAME, transcendentals=0
        ),
        name="filterbank",
    )(samples, window, table)


def correlate_kernel(pieces, blocks, *refs):
    place, own = refs[0], refs[1 : 1 + pieces]
    cols = refs[1 + pieces : 1 + pieces + blocks * pieces]
    out = refs[-1]
    shards, _, rows, _ = own[0].shape
    local = shards * pieces * rows
    lane = lax.broadcasted_iota(jnp.int32, (local, 256), 1)

    def gather(parts):
        return [jnp.stack([part[:, u] for part in parts], axis=1).reshape(local, LANES) for u in range(3)]

    mine = gather(own)
    rights = [gather(cols[n * pieces : (n + 1) * pieces]) for n in range(blocks)]
    for w in range(2):
        held = jnp.concatenate(mine[w : w + 2], axis=1).astype(jnp.float32)
        ahead, behind = pltpu.roll(held, 256 - NSPEC, 1), pltpu.roll(held, NSPEC, 1)
        left = []
        for i in range(2):
            start = w * 64 + i * PAIR
            real = (lane >= start) & (lane < start + NSPEC)
            imag = (lane >= start + NSPEC) & (lane < start + PAIR)
            left.append(jnp.where(real | imag, held, 0.0).astype(jnp.bfloat16))
            left.append(jnp.where(real, ahead, jnp.where(imag, -behind, 0.0)).astype(jnp.bfloat16))
        left = jnp.concatenate(left, axis=0)
        for n in range(blocks):
            right = jnp.concatenate(rights[n][w : w + 2], axis=1)
            term = lax.dot_general(left, right, (((1,), (1,)), ((), ())), preferred_element_type=jnp.float32)
            term = (term * (1.0 / NSPEC)).astype(jnp.bfloat16)
            at = pl.ds(pl.multiple_of(place[1 + n] * local, LANES), local)
            for i in range(2):
                for p in range(2):
                    k = 2 * i + p
                    out[p, 2 * w + i, :, at] = term[k * local : (k + 1) * local]


def correlate(place, own, cols, parts, before=None):
    pieces = len(own)
    blocks = len(cols) // pieces
    shards, tiles, rows, _ = own[0].shape
    local = shards * pieces * rows
    width = local * blocks
    three = pl.BlockSpec((shards, 3, rows, LANES), lambda i, place: (0, i, 0, 0))
    extra = [] if before is None else [before]
    operands = [place, *own, *cols, *extra]

    def body(*refs):
        return correlate_kernel(pieces, blocks, *refs[: 1 + pieces + len(cols)], refs[-1])

    return pl.pallas_call(
        body,
        grid_spec=pltpu.PrefetchScalarGridSpec(
            num_scalar_prefetch=1,
            grid=(CH_DEV // 4,),
            in_specs=[three] * (pieces + len(cols)) + [pl.BlockSpec(memory_space=pl.ANY)] * len(extra),
            out_specs=pl.BlockSpec((2, 4, local, width), lambda i, place: (0, i, 0, place[0])),
        ),
        out_shape=jax.ShapeDtypeStruct((2, CH_DEV, local, width * parts), jnp.bfloat16),
        input_output_aliases={len(operands) - 1: 0} if extra else {},
        compiler_params=pltpu.CompilerParams(vmem_limit_bytes=CORRELATE_VMEM),
        cost_estimate=pl.CostEstimate(
            flops=2 * 2 * CH_DEV * local * width * 256, bytes_accessed=2 * 2 * CH_DEV * local * width, transcendentals=0
        ),
        name="correlate",
    )(*operands)


def exchange(value, axis, distance):
    count = lax.axis_size(axis)
    return lax.ppermute(value, axis, [(i, i ^ distance) for i in range(count)])


def per_device(samples):
    antennas, length = samples.shape
    shards = lax.axis_size("freq")
    blocks = lax.axis_size("blk")
    channels = CH_DEV * shards
    frames = length // FRAME
    width = -(-channels // LANES) * LANES
    rows = 16 if antennas % 16 == 0 else 8
    pieces = antennas // rows
    window = jnp.asarray(make_window(FRAME, TAPS))
    table = jnp.asarray(make_table(FRAME, channels, width))
    tiled = samples.reshape(antennas // 8, 8, length // LANES, LANES).transpose(0, 2, 1, 3)
    tiled = tiled.reshape(antennas // 8, frames, FRAME // LANES, 8, LANES)
    own, near, far = [], [], []
    for piece in range(pieces):
        spectra = filterbank(tiled, window, table, piece, rows, shards)
        own.append(lax.all_to_all(spectra, "freq", split_axis=0, concat_axis=0, tiled=True))
        far.append(exchange(own[piece], "blk", 2))
        near.append(exchange(own[piece], "blk", 1))
    me = lax.axis_index("blk")

    def place(n):
        return jnp.stack([(me ^ n) >> 1, me & 1, (me & 1) ^ 1]).astype(jnp.int32)

    last = [exchange(value, "blk", 1) for value in far[:-1]]
    own, near, far[:-1], last = lax.optimization_barrier((own, near, far[:-1], last))
    result = correlate(place(0), own, own + near, blocks // 2)
    result, far[-1] = lax.optimization_barrier((result, far[-1]))
    last.append(exchange(far[-1], "blk", 1))
    return correlate(place(2), own, far + last, blocks // 2, result)


def solution(mesh):
    in_specs = (P(("blk", "freq"), None),)
    out_specs = P(None, "freq", "blk", None)
    return jax.shard_map(
        per_device, mesh=mesh, in_specs=in_specs, out_specs=out_specs, check_vma=False
    )
```

time: 79.9 us -> 70.3 us (0.88)
  local copies, waits for them, and re-layouts: 5.28 us -> 0 us
  waiting for transfers between devices: 13.7 us -> 11.3 us
  Pallas kernels: 43.2 us -> 41.7 us
    unnamed x8 -> x0, local copies, waits for them, and re-layouts: 5.28 us -> none
    ppermute x6, waiting for transfers between devices: 6.21 us -> 3.78 us  [exchange(): return lax.ppermute(value, axis, [(i, i ^ distance) for i in range(count)])]
    pallas_call x3 -> x4, Pallas kernels: 43.2 us -> 41.7 us  [the longest x2 31.6 us: filterbank(): pl.pallas_call(lambda *refs: filterbank_kernel(piece, rows, channels, wid...]
  transfers between devices with their start and end apart: 8 -> 8, of which waited for: 3 -> 3; matrix products, arithmetic and copies ran while one was open for 0% -> 0% of each run, Pallas kernels for 22% -> 30%
where the time goes in v2:
time: 70.3 us; the launch traced here: 70 us
  Pallas kernels  41.7 us (59%)
  starting transfers between devices  16.8 us (24%)
  waiting for transfers between devices  11.3 us (16%)
    pallas_call x2, Pallas kernels, filterbank(): pl.pallas_call(lambda *refs: filterbank_kernel(piece, rows, channels, wid...  31.6 us
    all_to_all x2, starting transfers between devices, per_device(): lax.all_to_all(spectra, 'freq', split_axis=0, concat_axis=0, tiled=True)  13.3 us
    pallas_call x2, Pallas kernels, correlate(): pl.pallas_call(body, grid_spec=pltpu.PrefetchScalarGridSpec(num_scalar_pr...  10.1 us
    all_to_all x2, waiting for transfers between devices, per_device(): lax.all_to_all(spectra, 'freq', split_axis=0, concat_axis=0, tiled=True)  7.52 us
    ppermute x6, waiting for transfers between devices, exchange(): return lax.ppermute(value, axis, [(i, i ^ distance) for i in range(count)])  3.78 us
    ppermute x6, starting transfers between devices, exchange(): return lax.ppermute(value, axis, [(i, i ^ distance) for i in range(count)])  3.5 us
  transfers between devices with their start and end apart: 8, of which 3 were waited for; matrix products, arithmetic and copies ran while one was open for 0% of the time, Pallas kernels for 30%

profile of v2, /device:TPU:0, one launch (start us, length us, event | category | flops | bytes accessed | tf_op | source)
XLA Modules:
  0.0 70.0 jit_solution(17365706854779122113)
XLA Ops:
  0.0 15.8 %filterbank.2 = bf16[8,9,16,128]{3,2,1,0:T(8,128)(2,1)} custom-call(s32[4,51,64,8,128]{4,3,2,1,0:T(8,128)} %bitcast.9, f32[4,8192]{1,0:T(4,128)} %constant.12.clone.refs_1_, bf16[8192,256]{1,0:T(8,128)(2,1)} %constant.13.clone.refs_2_), custom_call_target="tpu_custom_call" | custom-call | flops 3221225472 | bytes 26738688 | tf_op jit(solution)/shard_map/filterbank/pallas_call | solution.py:128
  15.8 7.3 %all-to-all-start = ((bf16[8,9,16,128]{3,2,1,0:T(8,128)(2,1)}), bf16[8,9,16,128]{3,2,1,0:T(8,128)(2,1)S(1)}, u32[]{:S(2)}, u32[]{:S(2)}) async-start(bf16[8,9,16,128]{3,2,1,0:T(8,128)(2,1)} %filterbank.2), calls=%async_computation | async-start | bytes 589824 | tf_op jit(solution)/shard_map/all_to_all | solution.py:241
  23.1 15.8 %filterbank.3 = bf16[8,9,16,128]{3,2,1,0:T(8,128)(2,1)} custom-call(s32[4,51,64,8,128]{4,3,2,1,0:T(8,128)} %bitcast.10, f32[4,8192]{1,0:T(4,128)} %constant.12.clone.refs_1_, bf16[8192,256]{1,0:T(8,128)(2,1)} %constant.13.clone.refs_2_), custom_call_target="tpu_custom_call" | custom-call | flops 3221225472 | bytes 26738688 | tf_op jit(solution)/shard_map/filterbank/pallas_call | solution.py:128
  38.9 0.0 all-to-all-done.refs_1_.refs_3_
  38.9 6.0 %all-to-all-start.1 = ((bf16[8,9,16,128]{3,2,1,0:T(8,128)(2,1)}), bf16[8,9,16,128]{3,2,1,0:T(8,128)(2,1)S(1)}, u32[]{:S(2)}, u32[]{:S(2)}) async-start(bf16[8,9,16,128]{3,2,1,0:T(8,128)(2,1)} %filterbank.3), calls=%async_computation.1 | async-start | bytes 589824 | tf_op jit(solution)/shard_map/all_to_all | solution.py:241
  44.9 1.5 %collective-permute-start.2 = (bf16[8,9,16,128]{3,2,1,0:T(8,128)(2,1)S(1)}, bf16[8,9,16,128]{3,2,1,0:T(8,128)(2,1)S(1)}, u32[]{:S(2)}, u32[]{:S(2)}) collective-permute-start(bf16[8,9,16,128]{3,2,1,0:T(8,128)(2,1)S(1)} %all-to-all-done.refs_1_.refs_3_), channel_id=1, source_target_pairs={{0,2},{1,3},{2,0},{3,1},{4,6},{5,7},{6,4},{7,5},{8,10},{9,11},{10,... | collective-permute-start | bytes 884744 | tf_op jit(solution)/shard_map/ppermute | solution.py:222
  46.4 0.0 collective-permute-start
  46.4 7.5 %all-to-all-done.1.refs_2_.refs_4_ = bf16[8,9,16,128]{3,2,1,0:T(8,128)(2,1)S(1)} async-done(((bf16[8,9,16,128]{3,2,1,0:T(8,128)(2,1)}), bf16[8,9,16,128]{3,2,1,0:T(8,128)(2,1)S(1)}, u32[]{:S(2)}, u32[]{:S(2)}) %all-to-all-start.1) | async-done | bytes 294944 | tf_op jit(solution)/shard_map/all_to_all | solution.py:241
  53.9 0.0 collective-permute-start.1
  53.9 0.0 collective-permute-done.2.refs_3_
  53.9 0.5 collective-permute-start.3
  54.4 1.5 %collective-permute-start.4 = (bf16[8,9,16,128]{3,2,1,0:T(8,128)(2,1)S(1)}, bf16[8,9,16,128]{3,2,1,0:T(8,128)(2,1)S(1)}, u32[]{:S(2)}, u32[]{:S(2)}) collective-permute-start(bf16[8,9,16,128]{3,2,1,0:T(8,128)(2,1)S(1)} %all-to-all-done.1.refs_2_.refs_4_), channel_id=1, source_target_pairs={{0,2},{1,3},{2,0},{3,1},{4,6},{5,7},{6,4},{7,5},{8,10},{9,11},{10,... | collective-permute-start | bytes 884744 | tf_op jit(solution)/shard_map/ppermute | solution.py:222
  55.9 0.1 add_add_fusion.1.refs_0_
  56.0 0.0 collective-permute-done.refs_5_
  56.0 0.0 collective-permute-done.1.refs_6_
  56.0 0.0 collective-permute-done.3.refs_5_
  56.0 5.1 %correlate.2.refs_7_ = bf16[2,12,256,1024]{3,2,1,0:T(8,128)(2,1)} custom-call(s32[3]{0:T(128)S(1)} %add_add_fusion.1.refs_0_, bf16[8,9,16,128]{3,2,1,0:T(8,128)(2,1)S(1)} %all-to-all-done.refs_1_.refs_3_, bf16[8,9,16,128]{3,2,1,0:T(8,128)(2,1)S(1)} %all-to-all-done.1.refs_2_.refs_4_, bf16[8,9,16,128]{3,2,1,0:T(8,128)(2,1)S(1)} %all-to-all-done.refs_1_.refs_3_, ...), custom_call_target="tpu_custom_call" | custom-call | flops 1610612736 | bytes 6291456 | tf_op jit(solution)/shard_map/correlate/pallas_call | solution.py:202
  61.1 2.3 %collective-permute-done.4.refs_4_ = bf16[8,9,16,128]{3,2,1,0:T(8,128)(2,1)S(1)} collective-permute-done((bf16[8,9,16,128]{3,2,1,0:T(8,128)(2,1)S(1)}, bf16[8,9,16,128]{3,2,1,0:T(8,128)(2,1)S(1)}, u32[]{:S(2)}, u32[]{:S(2)}) %collective-permute-start.4) | collective-permute-done | bytes 294944 | tf_op jit(solution)/shard_map/ppermute | solution.py:222
  63.3 0.0 collective-permute-start.5
  63.3 0.1 add_add_fusion.refs_0_
  63.4 1.5 %collective-permute-done.5.refs_6_ = bf16[8,9,16,128]{3,2,1,0:T(8,128)(2,1)S(1)} collective-permute-done((bf16[8,9,16,128]{3,2,1,0:T(8,128)(2,1)S(1)}, bf16[8,9,16,128]{3,2,1,0:T(8,128)(2,1)S(1)}, u32[]{:S(2)}, u32[]{:S(2)}) %collective-permute-start.5) | collective-permute-done | bytes 294944 | tf_op jit(solution)/shard_map/ppermute | solution.py:222
  64.9 5.1 %correlate.3 = bf16[2,12,256,1024]{3,2,1,0:T(8,128)(2,1)} custom-call(s32[3]{0:T(128)S(1)} %add_add_fusion.refs_0_, bf16[8,9,16,128]{3,2,1,0:T(8,128)(2,1)S(1)} %all-to-all-done.refs_1_.refs_3_, bf16[8,9,16,128]{3,2,1,0:T(8,128)(2,1)S(1)} %all-to-all-done.1.refs_2_.refs_4_, ...), custom_call_target="tpu_custom_call", output_to_operand_aliasing={{}: (7, {})} | custom-call | flops 1610612736 | bytes 6291456 | tf_op jit(solution)/shard_map/correlate/pallas_call | solution.py:202
Async XLA Ops:
  15.8 23.1 %all-to-all-start = ((bf16[8,9,16,128]{3,2,1,0:T(8,128)(2,1)}), bf16[8,9,16,128]{3,2,1,0:T(8,128)(2,1)S(1)}, u32[]{:S(2)}, u32[]{:S(2)}) async-start(bf16[8,9,16,128]{3,2,1,0:T(8,128)(2,1)} %filterbank.2), calls=%async_computation | async-start | bytes 589824 | tf_op jit(solution)/shard_map/all_to_all | solution.py:241
  38.9 15.0 %all-to-all-start.1 = ((bf16[8,9,16,128]{3,2,1,0:T(8,128)(2,1)}), bf16[8,9,16,128]{3,2,1,0:T(8,128)(2,1)S(1)}, u32[]{:S(2)}, u32[]{:S(2)}) async-start(bf16[8,9,16,128]{3,2,1,0:T(8,128)(2,1)} %filterbank.3), calls=%async_computation.1 | async-start | bytes 589824 | tf_op jit(solution)/shard_map/all_to_all | solution.py:241
  44.9 9.0 %collective-permute-start.2 = (bf16[8,9,16,128]{3,2,1,0:T(8,128)(2,1)S(1)}, bf16[8,9,16,128]{3,2,1,0:T(8,128)(2,1)S(1)}, u32[]{:S(2)}, u32[]{:S(2)}) collective-permute-start(bf16[8,9,16,128]{3,2,1,0:T(8,128)(2,1)S(1)} %all-to-all-done.refs_1_.refs_3_), channel_id=1, source_target_pairs={{0,2},{1,3},{2,0},{3,1},{4,6},{5,7},{6,4},{7,5},{8,10},{9,11},{10,... | collective-permute-start | bytes 884744 | tf_op jit(solution)/shard_map/ppermute | solution.py:222
  46.4 9.6 %collective-permute-start = (bf16[8,9,16,128]{3,2,1,0:T(8,128)(2,1)S(1)}, bf16[8,9,16,128]{3,2,1,0:T(8,128)(2,1)S(1)}, u32[]{:S(2)}, u32[]{:S(2)}) collective-permute-start(bf16[8,9,16,128]{3,2,1,0:T(8,128)(2,1)S(1)} %all-to-all-done.refs_1_.refs_3_), channel_id=1, source_target_pairs={{0,1},{1,0},{2,3},{3,2},{4,5},{5,4},{6,7},{7,6},{8,9},{9,8},{10,11... | collective-permute-start | bytes 884744 | tf_op jit(solution)/shard_map/ppermute | solution.py:222
  53.9 2.1 %collective-permute-start.1 = (bf16[8,9,16,128]{3,2,1,0:T(8,128)(2,1)S(1)}, bf16[8,9,16,128]{3,2,1,0:T(8,128)(2,1)S(1)}, u32[]{:S(2)}, u32[]{:S(2)}) collective-permute-start(bf16[8,9,16,128]{3,2,1,0:T(8,128)(2,1)S(1)} %all-to-all-done.1.refs_2_.refs_4_), channel_id=1, source_target_pairs={{0,1},{1,0},{2,3},{3,2},{4,5},{5,4},{6,7},{7,6},{8,9},{9,8},{10,11... | collective-permute-start | bytes 884744 | tf_op jit(solution)/shard_map/ppermute | solution.py:222
  53.9 2.1 %collective-permute-start.3 = (bf16[8,9,16,128]{3,2,1,0:T(8,128)(2,1)S(1)}, bf16[8,9,16,128]{3,2,1,0:T(8,128)(2,1)S(1)}, u32[]{:S(2)}, u32[]{:S(2)}) collective-permute-start(bf16[8,9,16,128]{3,2,1,0:T(8,128)(2,1)S(1)} %collective-permute-done.2.refs_3_), channel_id=1, source_target_pairs={{0,1},{1,0},{2,3},{3,2},{4,5},{5,4},{6,7},{7,6},{8,9},{9,8},{10,11... | collective-permute-start | bytes 884744 | tf_op jit(solution)/shard_map/ppermute | solution.py:222
  54.4 8.9 %collective-permute-start.4 = (bf16[8,9,16,128]{3,2,1,0:T(8,128)(2,1)S(1)}, bf16[8,9,16,128]{3,2,1,0:T(8,128)(2,1)S(1)}, u32[]{:S(2)}, u32[]{:S(2)}) collective-permute-start(bf16[8,9,16,128]{3,2,1,0:T(8,128)(2,1)S(1)} %all-to-all-done.1.refs_2_.refs_4_), channel_id=1, source_target_pairs={{0,2},{1,3},{2,0},{3,1},{4,6},{5,7},{6,4},{7,5},{8,10},{9,11},{10,... | collective-permute-start | bytes 884744 | tf_op jit(solution)/shard_map/ppermute | solution.py:222
  63.3 1.6 %collective-permute-start.5 = (bf16[8,9,16,128]{3,2,1,0:T(8,128)(2,1)S(1)}, bf16[8,9,16,128]{3,2,1,0:T(8,128)(2,1)S(1)}, u32[]{:S(2)}, u32[]{:S(2)}) collective-permute-start(bf16[8,9,16,128]{3,2,1,0:T(8,128)(2,1)S(1)} %collective-permute-done.4.refs_4_), channel_id=1, source_target_pairs={{0,1},{1,0},{2,3},{3,2},{4,5},{5,4},{6,7},{7,6},{8,9},{9,8},{10,11... | collective-permute-start | bytes 884744 | tf_op jit(solution)/shard_map/ppermute | solution.py:222

commit v3 on v2

--- a/solution.py
+++ b/solution.py
@@ -16,7 +16,7 @@
 LANES = 128
 PAIR = 2 * NSPEC
 BLOCK = 2048
-PARTS = ((0, 4), (4, 4), (8, 8), (16, 16), (32, 16), (48, 16))
+PARTS = ((0, 4), (4, 4), (8, 8), (16, 16), (32, 16), (48, 8), (56, 8))
 FILTER_VMEM = 60 * 1024 * 1024
 CORRELATE_VMEM = 32 * 1024 * 1024
 
@@ -26,7 +26,8 @@
     moment = np.arange(length, dtype=np.float64)
     offset = (moment + 0.5 - length / 2.0) / frame
     taper = 0.5 - 0.5 * np.cos(2.0 * math.pi * (moment + 0.5) / length)
-    return (np.sinc(offset) * taper).astype(np.float32).reshape(taps, frame)
+    w = (np.sinc(offset) * taper).astype(np.float32).reshape(taps, frame // LANES, 1, LANES)
+    return np.ascontiguousarray(np.broadcast_to(w, (taps, frame // LANES, 8, LANES)))
 
 
 def make_table(frame, channels, width):
@@ -40,7 +41,7 @@
     return table.astype(ml_dtypes.bfloat16)
 
 
-def filterbank_kernel(piece, rows, channels, width, x_hbm, w_ref, t_hbm, o_ref, x_ref, t_ref, filt, acc, turned, x_sem, t_sem):
+def filterbank_kernel(piece, rows, channels, width, x_hbm, w_hbm, t_hbm, o_hbm, x_ref, w_ref, t_ref, filt, acc, turned, o_ref, x_sem, w_sem, t_sem, o_sem):
     groups = rows // 8
     spec_rows = NSPEC * rows
     tiles = BLOCK // LANES
@@ -55,13 +56,21 @@
     def t_copy(b):
         return pltpu.make_async_copy(t_hbm.at[pl.ds(b * BLOCK, BLOCK)], t_ref.at[b], t_sem.at[b])
 
+    def o_copy(dest):
+        return pltpu.make_async_copy(o_ref.at[dest], o_hbm.at[dest], o_sem.at[dest])
+
+    def w_copy(n):
+        where = pl.ds(*PARTS[n])
+        return pltpu.make_async_copy(w_hbm.at[:, where], w_ref.at[:, where], w_sem.at[n])
+
     for n, (first, count) in enumerate(PARTS):
         x_copy(n).start()
+        w_copy(n).start()
         if (first + count) % tiles == 0:
             t_copy(first // tiles).start()
 
     def one_tile(tile, slot):
-        taps = [w_ref[pl.ds(k, 1), pl.ds(pl.multiple_of(tile * LANES, LANES), LANES)] for k in range(TAPS)]
+        taps = [w_ref[k, tile] for k in range(TAPS)]
         held = [[x_ref[g, f, tile].astype(jnp.float32) for f in range(TAPS - 1)] for g in range(groups)]
         ready = []
         for s in range(NSPEC):
@@ -79,13 +88,15 @@
 
     for n, (first, count) in enumerate(PARTS):
         x_copy(n).wait()
+        w_copy(n).wait()
         base = first % tiles
 
         def step(i, carry, first=first, base=base):
-            one_tile(first + i, base + i)
+            one_tile(first + 2 * i, base + 2 * i)
+            one_tile(first + 2 * i + 1, base + 2 * i + 1)
             return carry
 
-        lax.fori_loop(0, count, step, 0)
+        lax.fori_loop(0, count // 2, step, 0)
         if (first + count) % tiles:
             continue
         b = first // tiles
@@ -116,6 +127,10 @@
         for i in range(3):
             tile = jnp.where(lane < LANES - 32 * (i + 1), one[i], one[i + 1])
             o_ref[dest, place * 3 + i] = tile.astype(jnp.bfloat16)
+        if place == CH_DEV // 4 - 1:
+            o_copy(dest).start()
+    for dest in range(channels // CH_DEV):
+        o_copy(dest).wait()
 
 
 def filterbank(samples, window, table, piece, rows, shards):
@@ -129,19 +144,23 @@
         lambda *refs: filterbank_kernel(piece, rows, channels, width, *refs),
         in_specs=[
             pl.BlockSpec(memory_space=pl.ANY),
-            pl.BlockSpec(memory_space=pltpu.VMEM),
+            pl.BlockSpec(memory_space=pl.ANY),
             pl.BlockSpec(memory_space=pl.ANY),
         ],
-        out_specs=pl.BlockSpec(memory_space=pltpu.VMEM),
+        out_specs=pl.BlockSpec(memory_space=pl.ANY),
         out_shape=jax.ShapeDtypeStruct(shape, jnp.bfloat16),
         scratch_shapes=[
             pltpu.VMEM((groups, frames, FRAME // LANES, 8, LANES), jnp.int32),
+            pltpu.VMEM((TAPS, FRAME // LANES, 8, LANES), jnp.float32),
             pltpu.VMEM((FRAME // BLOCK, BLOCK, 2 * width), jnp.bfloat16),
             pltpu.VMEM((BLOCK // LANES, spec_rows, LANES), jnp.bfloat16),
             pltpu.VMEM((2 * width // LANES, spec_rows, LANES), jnp.float32),
             pltpu.VMEM((channels * rows, LANES), jnp.float32),
+            pltpu.VMEM(shape, jnp.bfloat16),
+            pltpu.SemaphoreType.DMA((len(PARTS),)),
             pltpu.SemaphoreType.DMA((len(PARTS),)),
             pltpu.SemaphoreType.DMA((FRAME // BLOCK,)),
+            pltpu.SemaphoreType.DMA((shards,)),
         ],
         compiler_params=pltpu.CompilerParams(vmem_limit_bytes=FILTER_VMEM),
         cost_estimate=pl.CostEstimate(
@@ -154,18 +173,24 @@
 def correlate_kernel(pieces, blocks, *refs):
     place, own = refs[0], refs[1 : 1 + pieces]
     cols = refs[1 + pieces : 1 + pieces + blocks * pieces]
-    out = refs[-1]
+    out, stage, sem = refs[-3:]
     shards, _, rows, _ = own[0].shape
     local = shards * pieces * rows
+    width = blocks * local
     lane = lax.broadcasted_iota(jnp.int32, (local, 256), 1)
-
-    def gather(parts):
-        return [jnp.stack([part[:, u] for part in parts], axis=1).reshape(local, LANES) for u in range(3)]
-
-    mine = gather(own)
-    rights = [gather(cols[n * pieces : (n + 1) * pieces]) for n in range(blocks)]
-    for w in range(2):
-        held = jnp.concatenate(mine[w : w + 2], axis=1).astype(jnp.float32)
+    at = [pl.ds(pl.multiple_of(place[1 + n] * local, LANES), local) for n in range(blocks)]
+    goal = pl.ds(pl.multiple_of(place[0] * width, LANES), width)
+
+    def gather(parts, tile):
+        halves = [jnp.stack([part[:, tile + u] for part in parts], axis=1).reshape(local, LANES) for u in range(2)]
+        return jnp.concatenate(halves, axis=1)
+
+    def copy(pair):
+        return pltpu.make_async_copy(stage.at[pair], out.at[:, pl.ds(2 * pair, 2), :, goal], sem.at[pair])
+
+    for pair in range(CH_DEV // 2):
+        q, w = pair // 2, pair % 2
+        held = gather(own, 3 * q + w).astype(jnp.float32)
         ahead, behind = pltpu.roll(held, 256 - NSPEC, 1), pltpu.roll(held, NSPEC, 1)
         left = []
         for i in range(2):
@@ -176,14 +201,16 @@
             left.append(jnp.where(real, ahead, jnp.where(imag, -behind, 0.0)).astype(jnp.bfloat16))
         left = jnp.concatenate(left, axis=0)
         for n in range(blocks):
-            right = jnp.concatenate(rights[n][w : w + 2], axis=1)
+            right = gather(cols[n * pieces : (n + 1) * pieces], 3 * q + w)
             term = lax.dot_general(left, right, (((1,), (1,)), ((), ())), preferred_element_type=jnp.float32)
             term = (term * (1.0 / NSPEC)).astype(jnp.bfloat16)
-            at = pl.ds(pl.multiple_of(place[1 + n] * local, LANES), local)
             for i in range(2):
                 for p in range(2):
                     k = 2 * i + p
-                    out[p, 2 * w + i, :, at] = term[k * local : (k + 1) * local]
+                    stage[pair, p, i, :, at[n]] = term[k * local : (k + 1) * local]
+        copy(pair).start()
+    for pair in range(CH_DEV // 2):
+        copy(pair).wait()
 
 
 def correlate(place, own, cols, parts, before=None):
@@ -192,22 +219,23 @@
     shards, tiles, rows, _ = own[0].shape
     local = shards * pieces * rows
     width = local * blocks
-    three = pl.BlockSpec((shards, 3, rows, LANES), lambda i, place: (0, i, 0, 0))
     extra = [] if before is None else [before]
     operands = [place, *own, *cols, *extra]
+    here = pl.BlockSpec(memory_space=pltpu.VMEM)
+    far = pl.BlockSpec(memory_space=pl.ANY)
 
     def body(*refs):
-        return correlate_kernel(pieces, blocks, *refs[: 1 + pieces + len(cols)], refs[-1])
+        return correlate_kernel(pieces, blocks, *refs[: 1 + pieces + len(cols)], *refs[-3:])
 
     return pl.pallas_call(
         body,
-        grid_spec=pltpu.PrefetchScalarGridSpec(
-            num_scalar_prefetch=1,
-            grid=(CH_DEV // 4,),
-            in_specs=[three] * (pieces + len(cols)) + [pl.BlockSpec(memory_space=pl.ANY)] * len(extra),
-            out_specs=pl.BlockSpec((2, 4, local, width), lambda i, place: (0, i, 0, place[0])),
-        ),
+        in_specs=[pl.BlockSpec(memory_space=pltpu.SMEM)] + [here] * (pieces + len(cols)) + [far] * len(extra),
+        out_specs=far,
         out_shape=jax.ShapeDtypeStruct((2, CH_DEV, local, width * parts), jnp.bfloat16),
+        scratch_shapes=[
+            pltpu.VMEM((CH_DEV // 2, 2, 2, local, width), jnp.bfloat16),
+            pltpu.SemaphoreType.DMA((CH_DEV // 2,)),
+        ],
         input_output_aliases={len(operands) - 1: 0} if extra else {},
         compiler_params=pltpu.CompilerParams(vmem_limit_bytes=CORRELATE_VMEM),
         cost_estimate=pl.CostEstimate(

time: 70.3 us -> 68.1 us (0.969)
  Pallas kernels: 41.7 us -> 38.9 us
    pallas_call x2, Pallas kernels: 31.6 us -> 29.6 us  [filterbank(): pl.pallas_call(lambda *refs: filterbank_kernel(piece, rows, channels, wid...]
    pallas_call x2, Pallas kernels: 10.1 us -> 9.36 us  [correlate(): pl.pallas_call(body, in_specs=[pl.BlockSpec(memory_space=pltpu.SMEM)] + [...]
  transfers between devices with their start and end apart: 8 -> 8, of which waited for: 3 -> 3; matrix products, arithmetic and copies ran while one was open for 0% -> 0% of each run, Pallas kernels for 30% -> 29%
where the time goes in v3:
time: 68.1 us; the launch traced here: 67.8 us
  Pallas kernels  38.9 us (57%)
  starting transfers between devices  16.8 us (25%)
  waiting for transfers between devices  11.7 us (17%)
    pallas_call x2, Pallas kernels, filterbank(): pl.pallas_call(lambda *refs: filterbank_kernel(piece, rows, channels, wid...  29.6 us
    all_to_all x2, starting transfers between devices, per_device(): lax.all_to_all(spectra, 'freq', split_axis=0, concat_axis=0, tiled=True)  13.3 us
    pallas_call x2, Pallas kernels, correlate(): pl.pallas_call(body, in_specs=[pl.BlockSpec(memory_space=pltpu.SMEM)] + [...  9.36 us
    all_to_all x2, waiting for transfers between devices, per_device(): lax.all_to_all(spectra, 'freq', split_axis=0, concat_axis=0, tiled=True)  7.52 us
    ppermute x6, waiting for transfers between devices, exchange(): return lax.ppermute(value, axis, [(i, i ^ distance) for i in range(count)])  4.16 us
    ppermute x6, starting transfers between devices, exchange(): return lax.ppermute(value, axis, [(i, i ^ distance) for i in range(count)])  3.5 us
  transfers between devices with their start and end apart: 8, of which 3 were waited for; matrix products, arithmetic and copies ran while one was open for 0% of the time, Pallas kernels for 29%

profile of v3, /device:TPU:0, one launch (start us, length us, event | category | flops | bytes accessed | tf_op | source)
XLA Modules:
  0.0 67.8 jit_solution(9841982631243540095)
XLA Ops:
  0.0 14.8 %filterbank.2 = bf16[8,9,16,128]{3,2,1,0:T(8,128)(2,1)} custom-call(s32[4,51,64,8,128]{4,3,2,1,0:T(8,128)} %bitcast.9, f32[4,64,8,128]{3,2,1,0:T(8,128)} %constant.12.clone.refs_1_, bf16[8192,256]{1,0:T(8,128)(2,1)} %constant.13.clone.refs_2_), custom_call_target="tpu_custom_call" | custom-call | flops 3221225472 | bytes 26738688 | tf_op jit(solution)/shard_map/filterbank/pallas_call | solution.py:143
  14.8 7.3 %all-to-all-start = ((bf16[8,9,16,128]{3,2,1,0:T(8,128)(2,1)}), bf16[8,9,16,128]{3,2,1,0:T(8,128)(2,1)S(1)}, u32[]{:S(2)}, u32[]{:S(2)}) async-start(bf16[8,9,16,128]{3,2,1,0:T(8,128)(2,1)} %filterbank.2), calls=%async_computation | async-start | bytes 589824 | tf_op jit(solution)/shard_map/all_to_all | solution.py:269
  22.1 14.8 %filterbank.3 = bf16[8,9,16,128]{3,2,1,0:T(8,128)(2,1)} custom-call(s32[4,51,64,8,128]{4,3,2,1,0:T(8,128)} %bitcast.10, f32[4,64,8,128]{3,2,1,0:T(8,128)} %constant.12.clone.refs_1_, bf16[8192,256]{1,0:T(8,128)(2,1)} %constant.13.clone.refs_2_), custom_call_target="tpu_custom_call" | custom-call | flops 3221225472 | bytes 26738688 | tf_op jit(solution)/shard_map/filterbank/pallas_call | solution.py:143
  36.9 0.0 all-to-all-done.refs_1_.refs_3_
  36.9 6.0 %all-to-all-start.1 = ((bf16[8,9,16,128]{3,2,1,0:T(8,128)(2,1)}), bf16[8,9,16,128]{3,2,1,0:T(8,128)(2,1)S(1)}, u32[]{:S(2)}, u32[]{:S(2)}) async-start(bf16[8,9,16,128]{3,2,1,0:T(8,128)(2,1)} %filterbank.3), calls=%async_computation.1 | async-start | bytes 589824 | tf_op jit(solution)/shard_map/all_to_all | solution.py:269
  42.9 1.5 %collective-permute-start.2 = (bf16[8,9,16,128]{3,2,1,0:T(8,128)(2,1)S(1)}, bf16[8,9,16,128]{3,2,1,0:T(8,128)(2,1)S(1)}, u32[]{:S(2)}, u32[]{:S(2)}) collective-permute-start(bf16[8,9,16,128]{3,2,1,0:T(8,128)(2,1)S(1)} %all-to-all-done.refs_1_.refs_3_), channel_id=1, source_target_pairs={{0,2},{1,3},{2,0},{3,1},{4,6},{5,7},{6,4},{7,5},{8,10},{9,11},{10,... | collective-permute-start | bytes 884744 | tf_op jit(solution)/shard_map/ppermute | solution.py:250
  44.4 0.0 collective-permute-start
  44.4 7.5 %all-to-all-done.1.refs_2_.refs_4_ = bf16[8,9,16,128]{3,2,1,0:T(8,128)(2,1)S(1)} async-done(((bf16[8,9,16,128]{3,2,1,0:T(8,128)(2,1)}), bf16[8,9,16,128]{3,2,1,0:T(8,128)(2,1)S(1)}, u32[]{:S(2)}, u32[]{:S(2)}) %all-to-all-start.1) | async-done | bytes 294944 | tf_op jit(solution)/shard_map/all_to_all | solution.py:269
  51.9 0.0 collective-permute-start.1
  51.9 0.0 collective-permute-done.2.refs_3_
  51.9 0.5 collective-permute-start.3
  52.4 1.5 %collective-permute-start.4 = (bf16[8,9,16,128]{3,2,1,0:T(8,128)(2,1)S(1)}, bf16[8,9,16,128]{3,2,1,0:T(8,128)(2,1)S(1)}, u32[]{:S(2)}, u32[]{:S(2)}) collective-permute-start(bf16[8,9,16,128]{3,2,1,0:T(8,128)(2,1)S(1)} %all-to-all-done.1.refs_2_.refs_4_), channel_id=1, source_target_pairs={{0,2},{1,3},{2,0},{3,1},{4,6},{5,7},{6,4},{7,5},{8,10},{9,11},{10,... | collective-permute-start | bytes 884744 | tf_op jit(solution)/shard_map/ppermute | solution.py:250
  53.9 0.1 add_add_fusion.1.refs_0_
  54.0 0.0 collective-permute-done.refs_5_
  54.0 0.0 collective-permute-done.1.refs_6_
  54.0 0.0 collective-permute-done.3.refs_5_
  54.0 4.7 %correlate.2.refs_7_ = bf16[2,12,256,1024]{3,2,1,0:T(8,128)(2,1)} custom-call(s32[3]{0:T(128)S(1)} %add_add_fusion.1.refs_0_, bf16[8,9,16,128]{3,2,1,0:T(8,128)(2,1)S(1)} %all-to-all-done.refs_1_.refs_3_, bf16[8,9,16,128]{3,2,1,0:T(8,128)(2,1)S(1)} %all-to-all-done.1.refs_2_.refs_4_, bf16[8,9,16,128]{3,2,1,0:T(8,128)(2,1)S(1)} %all-to-all-done.refs_1_.refs_3_, ...), custom_call_target="tpu_custom_call" | custom-call | flops 1610612736 | bytes 6291456 | tf_op jit(solution)/shard_map/correlate/pallas_call | solution.py:230
  58.7 2.6 %collective-permute-done.4.refs_4_ = bf16[8,9,16,128]{3,2,1,0:T(8,128)(2,1)S(1)} collective-permute-done((bf16[8,9,16,128]{3,2,1,0:T(8,128)(2,1)S(1)}, bf16[8,9,16,128]{3,2,1,0:T(8,128)(2,1)S(1)}, u32[]{:S(2)}, u32[]{:S(2)}) %collective-permute-start.4) | collective-permute-done | bytes 294944 | tf_op jit(solution)/shard_map/ppermute | solution.py:250
  61.4 0.0 collective-permute-start.5
  61.4 0.1 add_add_fusion.refs_0_
  61.4 1.5 %collective-permute-done.5.refs_6_ = bf16[8,9,16,128]{3,2,1,0:T(8,128)(2,1)S(1)} collective-permute-done((bf16[8,9,16,128]{3,2,1,0:T(8,128)(2,1)S(1)}, bf16[8,9,16,128]{3,2,1,0:T(8,128)(2,1)S(1)}, u32[]{:S(2)}, u32[]{:S(2)}) %collective-permute-start.5) | collective-permute-done | bytes 294944 | tf_op jit(solution)/shard_map/ppermute | solution.py:250
  62.9 4.7 %correlate.3 = bf16[2,12,256,1024]{3,2,1,0:T(8,128)(2,1)} custom-call(s32[3]{0:T(128)S(1)} %add_add_fusion.refs_0_, bf16[8,9,16,128]{3,2,1,0:T(8,128)(2,1)S(1)} %all-to-all-done.refs_1_.refs_3_, bf16[8,9,16,128]{3,2,1,0:T(8,128)(2,1)S(1)} %all-to-all-done.1.refs_2_.refs_4_, ...), custom_call_target="tpu_custom_call", output_to_operand_aliasing={{}: (7, {})} | custom-call | flops 1610612736 | bytes 6291456 | tf_op jit(solution)/shard_map/correlate/pallas_call | solution.py:230
Async XLA Ops:
  14.8 22.1 %all-to-all-start = ((bf16[8,9,16,128]{3,2,1,0:T(8,128)(2,1)}), bf16[8,9,16,128]{3,2,1,0:T(8,128)(2,1)S(1)}, u32[]{:S(2)}, u32[]{:S(2)}) async-start(bf16[8,9,16,128]{3,2,1,0:T(8,128)(2,1)} %filterbank.2), calls=%async_computation | async-start | bytes 589824 | tf_op jit(solution)/shard_map/all_to_all | solution.py:269
  36.9 15.0 %all-to-all-start.1 = ((bf16[8,9,16,128]{3,2,1,0:T(8,128)(2,1)}), bf16[8,9,16,128]{3,2,1,0:T(8,128)(2,1)S(1)}, u32[]{:S(2)}, u32[]{:S(2)}) async-start(bf16[8,9,16,128]{3,2,1,0:T(8,128)(2,1)} %filterbank.3), calls=%async_computation.1 | async-start | bytes 589824 | tf_op jit(solution)/shard_map/all_to_all | solution.py:269
  42.9 9.0 %collective-permute-start.2 = (bf16[8,9,16,128]{3,2,1,0:T(8,128)(2,1)S(1)}, bf16[8,9,16,128]{3,2,1,0:T(8,128)(2,1)S(1)}, u32[]{:S(2)}, u32[]{:S(2)}) collective-permute-start(bf16[8,9,16,128]{3,2,1,0:T(8,128)(2,1)S(1)} %all-to-all-done.refs_1_.refs_3_), channel_id=1, source_target_pairs={{0,2},{1,3},{2,0},{3,1},{4,6},{5,7},{6,4},{7,5},{8,10},{9,11},{10,... | collective-permute-start | bytes 884744 | tf_op jit(solution)/shard_map/ppermute | solution.py:250
  44.4 9.6 %collective-permute-start = (bf16[8,9,16,128]{3,2,1,0:T(8,128)(2,1)S(1)}, bf16[8,9,16,128]{3,2,1,0:T(8,128)(2,1)S(1)}, u32[]{:S(2)}, u32[]{:S(2)}) collective-permute-start(bf16[8,9,16,128]{3,2,1,0:T(8,128)(2,1)S(1)} %all-to-all-done.refs_1_.refs_3_), channel_id=1, source_target_pairs={{0,1},{1,0},{2,3},{3,2},{4,5},{5,4},{6,7},{7,6},{8,9},{9,8},{10,11... | collective-permute-start | bytes 884744 | tf_op jit(solution)/shard_map/ppermute | solution.py:250
  51.9 2.1 %collective-permute-start.1 = (bf16[8,9,16,128]{3,2,1,0:T(8,128)(2,1)S(1)}, bf16[8,9,16,128]{3,2,1,0:T(8,128)(2,1)S(1)}, u32[]{:S(2)}, u32[]{:S(2)}) collective-permute-start(bf16[8,9,16,128]{3,2,1,0:T(8,128)(2,1)S(1)} %all-to-all-done.1.refs_2_.refs_4_), channel_id=1, source_target_pairs={{0,1},{1,0},{2,3},{3,2},{4,5},{5,4},{6,7},{7,6},{8,9},{9,8},{10,11... | collective-permute-start | bytes 884744 | tf_op jit(solution)/shard_map/ppermute | solution.py:250
  51.9 2.1 %collective-permute-start.3 = (bf16[8,9,16,128]{3,2,1,0:T(8,128)(2,1)S(1)}, bf16[8,9,16,128]{3,2,1,0:T(8,128)(2,1)S(1)}, u32[]{:S(2)}, u32[]{:S(2)}) collective-permute-start(bf16[8,9,16,128]{3,2,1,0:T(8,128)(2,1)S(1)} %collective-permute-done.2.refs_3_), channel_id=1, source_target_pairs={{0,1},{1,0},{2,3},{3,2},{4,5},{5,4},{6,7},{7,6},{8,9},{9,8},{10,11... | collective-permute-start | bytes 884744 | tf_op jit(solution)/shard_map/ppermute | solution.py:250
  52.4 8.9 %collective-permute-start.4 = (bf16[8,9,16,128]{3,2,1,0:T(8,128)(2,1)S(1)}, bf16[8,9,16,128]{3,2,1,0:T(8,128)(2,1)S(1)}, u32[]{:S(2)}, u32[]{:S(2)}) collective-permute-start(bf16[8,9,16,128]{3,2,1,0:T(8,128)(2,1)S(1)} %all-to-all-done.1.refs_2_.refs_4_), channel_id=1, source_target_pairs={{0,2},{1,3},{2,0},{3,1},{4,6},{5,7},{6,4},{7,5},{8,10},{9,11},{10,... | collective-permute-start | bytes 884744 | tf_op jit(solution)/shard_map/ppermute | solution.py:250
  61.4 1.6 %collective-permute-start.5 = (bf16[8,9,16,128]{3,2,1,0:T(8,128)(2,1)S(1)}, bf16[8,9,16,128]{3,2,1,0:T(8,128)(2,1)S(1)}, u32[]{:S(2)}, u32[]{:S(2)}) collective-permute-start(bf16[8,9,16,128]{3,2,1,0:T(8,128)(2,1)S(1)} %collective-permute-done.4.refs_4_), channel_id=1, source_target_pairs={{0,1},{1,0},{2,3},{3,2},{4,5},{5,4},{6,7},{7,6},{8,9},{9,8},{10,11... | collective-permute-start | bytes 884744 | tf_op jit(solution)/shard_map/ppermute | solution.py:250

commit v4 on v3

--- a/solution.py
+++ b/solution.py
@@ -92,11 +92,11 @@
         base = first % tiles
 
         def step(i, carry, first=first, base=base):
-            one_tile(first + 2 * i, base + 2 * i)
-            one_tile(first + 2 * i + 1, base + 2 * i + 1)
+            for u in range(4):
+                one_tile(first + 4 * i + u, base + 4 * i + u)
             return carry
 
-        lax.fori_loop(0, count // 2, step, 0)
+        lax.fori_loop(0, count // 4, step, 0)
         if (first + count) % tiles:
             continue
         b = first // tiles
@@ -199,15 +199,14 @@
             imag = (lane >= start + NSPEC) & (lane < start + PAIR)
             left.append(jnp.where(real | imag, held, 0.0).astype(jnp.bfloat16))
             left.append(jnp.where(real, ahead, jnp.where(imag, -behind, 0.0)).astype(jnp.bfloat16))
-        left = jnp.concatenate(left, axis=0)
         for n in range(blocks):
             right = gather(cols[n * pieces : (n + 1) * pieces], 3 * q + w)
-            term = lax.dot_general(left, right, (((1,), (1,)), ((), ())), preferred_element_type=jnp.float32)
-            term = (term * (1.0 / NSPEC)).astype(jnp.bfloat16)
             for i in range(2):
                 for p in range(2):
-                    k = 2 * i + p
-                    stage[pair, p, i, :, at[n]] = term[k * local : (k + 1) * local]
+                    term = lax.dot_general(
+                        left[2 * i + p], right, (((1,), (1,)), ((), ())), preferred_element_type=jnp.float32
+                    )
+                    stage[pair, p, i, :, at[n]] = (term * (1.0 / NSPEC)).astype(jnp.bfloat16)
         copy(pair).start()
     for pair in range(CH_DEV // 2):
         copy(pair).wait()

time: 68.1 us -> 67.7 us (level)
  transfers between devices with their start and end apart: 8 -> 8, of which waited for: 3 -> 3; matrix products, arithmetic and copies ran while one was open for 0% -> 0% of each run, Pallas kernels for 29% -> 28%
where the time goes in v4:
time: 67.7 us; the launch traced here: 67.4 us
  Pallas kernels  38.4 us (57%)
  starting transfers between devices  16.8 us (25%)
  waiting for transfers between devices  11.9 us (18%)
    pallas_call x2, Pallas kernels, filterbank(): pl.pallas_call(lambda *refs: filterbank_kernel(piece, rows, channels, wid...  29.4 us
    all_to_all x2, starting transfers between devices, per_device(): lax.all_to_all(spectra, 'freq', split_axis=0, concat_axis=0, tiled=True)  13.3 us
    pallas_call x2, Pallas kernels, correlate(): pl.pallas_call(body, in_specs=[pl.BlockSpec(memory_space=pltpu.SMEM)] + [...  9.02 us
    all_to_all x2, waiting for transfers between devices, per_device(): lax.all_to_all(spectra, 'freq', split_axis=0, concat_axis=0, tiled=True)  7.52 us
    ppermute x6, waiting for transfers between devices, exchange(): return lax.ppermute(value, axis, [(i, i ^ distance) for i in range(count)])  4.33 us
    ppermute x6, starting transfers between devices, exchange(): return lax.ppermute(value, axis, [(i, i ^ distance) for i in range(count)])  3.5 us
  transfers between devices with their start and end apart: 8, of which 3 were waited for; matrix products, arithmetic and copies ran while one was open for 0% of the time, Pallas kernels for 28%

profile of v4, /device:TPU:0, one launch (start us, length us, event | category | flops | bytes accessed | tf_op | source)
XLA Modules:
  0.0 67.4 jit_solution(4973762725134714566)
XLA Ops:
  0.0 14.7 %filterbank.2 = bf16[8,9,16,128]{3,2,1,0:T(8,128)(2,1)} custom-call(s32[4,51,64,8,128]{4,3,2,1,0:T(8,128)} %bitcast.9, f32[4,64,8,128]{3,2,1,0:T(8,128)} %constant.12.clone.refs_1_, bf16[8192,256]{1,0:T(8,128)(2,1)} %constant.13.clone.refs_2_), custom_call_target="tpu_custom_call" | custom-call | flops 3221225472 | bytes 26738688 | tf_op jit(solution)/shard_map/filterbank/pallas_call | solution.py:143
  14.7 7.3 %all-to-all-start = ((bf16[8,9,16,128]{3,2,1,0:T(8,128)(2,1)}), bf16[8,9,16,128]{3,2,1,0:T(8,128)(2,1)S(1)}, u32[]{:S(2)}, u32[]{:S(2)}) async-start(bf16[8,9,16,128]{3,2,1,0:T(8,128)(2,1)} %filterbank.2), calls=%async_computation | async-start | bytes 589824 | tf_op jit(solution)/shard_map/all_to_all | solution.py:268
  22.0 14.7 %filterbank.3 = bf16[8,9,16,128]{3,2,1,0:T(8,128)(2,1)} custom-call(s32[4,51,64,8,128]{4,3,2,1,0:T(8,128)} %bitcast.10, f32[4,64,8,128]{3,2,1,0:T(8,128)} %constant.12.clone.refs_1_, bf16[8192,256]{1,0:T(8,128)(2,1)} %constant.13.clone.refs_2_), custom_call_target="tpu_custom_call" | custom-call | flops 3221225472 | bytes 26738688 | tf_op jit(solution)/shard_map/filterbank/pallas_call | solution.py:143
  36.7 0.0 all-to-all-done.refs_1_.refs_3_
  36.7 6.0 %all-to-all-start.1 = ((bf16[8,9,16,128]{3,2,1,0:T(8,128)(2,1)}), bf16[8,9,16,128]{3,2,1,0:T(8,128)(2,1)S(1)}, u32[]{:S(2)}, u32[]{:S(2)}) async-start(bf16[8,9,16,128]{3,2,1,0:T(8,128)(2,1)} %filterbank.3), calls=%async_computation.1 | async-start | bytes 589824 | tf_op jit(solution)/shard_map/all_to_all | solution.py:268
  42.7 1.5 %collective-permute-start.2 = (bf16[8,9,16,128]{3,2,1,0:T(8,128)(2,1)S(1)}, bf16[8,9,16,128]{3,2,1,0:T(8,128)(2,1)S(1)}, u32[]{:S(2)}, u32[]{:S(2)}) collective-permute-start(bf16[8,9,16,128]{3,2,1,0:T(8,128)(2,1)S(1)} %all-to-all-done.refs_1_.refs_3_), channel_id=1, source_target_pairs={{0,2},{1,3},{2,0},{3,1},{4,6},{5,7},{6,4},{7,5},{8,10},{9,11},{10,... | collective-permute-start | bytes 884744 | tf_op jit(solution)/shard_map/ppermute | solution.py:249
  44.2 0.0 collective-permute-start
  44.2 7.5 %all-to-all-done.1.refs_2_.refs_4_ = bf16[8,9,16,128]{3,2,1,0:T(8,128)(2,1)S(1)} async-done(((bf16[8,9,16,128]{3,2,1,0:T(8,128)(2,1)}), bf16[8,9,16,128]{3,2,1,0:T(8,128)(2,1)S(1)}, u32[]{:S(2)}, u32[]{:S(2)}) %all-to-all-start.1) | async-done | bytes 294944 | tf_op jit(solution)/shard_map/all_to_all | solution.py:268
  51.7 0.0 collective-permute-start.1
  51.7 0.0 collective-permute-done.2.refs_3_
  51.7 0.5 collective-permute-start.3
  52.2 1.5 %collective-permute-start.4 = (bf16[8,9,16,128]{3,2,1,0:T(8,128)(2,1)S(1)}, bf16[8,9,16,128]{3,2,1,0:T(8,128)(2,1)S(1)}, u32[]{:S(2)}, u32[]{:S(2)}) collective-permute-start(bf16[8,9,16,128]{3,2,1,0:T(8,128)(2,1)S(1)} %all-to-all-done.1.refs_2_.refs_4_), channel_id=1, source_target_pairs={{0,2},{1,3},{2,0},{3,1},{4,6},{5,7},{6,4},{7,5},{8,10},{9,11},{10,... | collective-permute-start | bytes 884744 | tf_op jit(solution)/shard_map/ppermute | solution.py:249
  53.7 0.1 add_add_fusion.1.refs_0_
  53.8 0.0 collective-permute-done.refs_5_
  53.8 0.0 collective-permute-done.1.refs_6_
  53.8 0.0 collective-permute-done.3.refs_5_
  53.8 4.5 %correlate.2.refs_7_ = bf16[2,12,256,1024]{3,2,1,0:T(8,128)(2,1)} custom-call(s32[3]{0:T(128)S(1)} %add_add_fusion.1.refs_0_, bf16[8,9,16,128]{3,2,1,0:T(8,128)(2,1)S(1)} %all-to-all-done.refs_1_.refs_3_, bf16[8,9,16,128]{3,2,1,0:T(8,128)(2,1)S(1)} %all-to-all-done.1.refs_2_.refs_4_, bf16[8,9,16,128]{3,2,1,0:T(8,128)(2,1)S(1)} %all-to-all-done.refs_1_.refs_3_, ...), custom_call_target="tpu_custom_call" | custom-call | flops 1610612736 | bytes 6291456 | tf_op jit(solution)/shard_map/correlate/pallas_call | solution.py:229
  58.3 2.8 %collective-permute-done.4.refs_4_ = bf16[8,9,16,128]{3,2,1,0:T(8,128)(2,1)S(1)} collective-permute-done((bf16[8,9,16,128]{3,2,1,0:T(8,128)(2,1)S(1)}, bf16[8,9,16,128]{3,2,1,0:T(8,128)(2,1)S(1)}, u32[]{:S(2)}, u32[]{:S(2)}) %collective-permute-start.4) | collective-permute-done | bytes 294944 | tf_op jit(solution)/shard_map/ppermute | solution.py:249
  61.2 0.0 collective-permute-start.5
  61.2 0.1 add_add_fusion.refs_0_
  61.2 1.5 %collective-permute-done.5.refs_6_ = bf16[8,9,16,128]{3,2,1,0:T(8,128)(2,1)S(1)} collective-permute-done((bf16[8,9,16,128]{3,2,1,0:T(8,128)(2,1)S(1)}, bf16[8,9,16,128]{3,2,1,0:T(8,128)(2,1)S(1)}, u32[]{:S(2)}, u32[]{:S(2)}) %collective-permute-start.5) | collective-permute-done | bytes 294944 | tf_op jit(solution)/shard_map/ppermute | solution.py:249
  62.7 4.5 %correlate.3 = bf16[2,12,256,1024]{3,2,1,0:T(8,128)(2,1)} custom-call(s32[3]{0:T(128)S(1)} %add_add_fusion.refs_0_, bf16[8,9,16,128]{3,2,1,0:T(8,128)(2,1)S(1)} %all-to-all-done.refs_1_.refs_3_, bf16[8,9,16,128]{3,2,1,0:T(8,128)(2,1)S(1)} %all-to-all-done.1.refs_2_.refs_4_, ...), custom_call_target="tpu_custom_call", output_to_operand_aliasing={{}: (7, {})} | custom-call | flops 1610612736 | bytes 6291456 | tf_op jit(solution)/shard_map/correlate/pallas_call | solution.py:229
Async XLA Ops:
  14.7 22.0 %all-to-all-start = ((bf16[8,9,16,128]{3,2,1,0:T(8,128)(2,1)}), bf16[8,9,16,128]{3,2,1,0:T(8,128)(2,1)S(1)}, u32[]{:S(2)}, u32[]{:S(2)}) async-start(bf16[8,9,16,128]{3,2,1,0:T(8,128)(2,1)} %filterbank.2), calls=%async_computation | async-start | bytes 589824 | tf_op jit(solution)/shard_map/all_to_all | solution.py:268
  36.7 15.0 %all-to-all-start.1 = ((bf16[8,9,16,128]{3,2,1,0:T(8,128)(2,1)}), bf16[8,9,16,128]{3,2,1,0:T(8,128)(2,1)S(1)}, u32[]{:S(2)}, u32[]{:S(2)}) async-start(bf16[8,9,16,128]{3,2,1,0:T(8,128)(2,1)} %filterbank.3), calls=%async_computation.1 | async-start | bytes 589824 | tf_op jit(solution)/shard_map/all_to_all | solution.py:268
  42.7 9.0 %collective-permute-start.2 = (bf16[8,9,16,128]{3,2,1,0:T(8,128)(2,1)S(1)}, bf16[8,9,16,128]{3,2,1,0:T(8,128)(2,1)S(1)}, u32[]{:S(2)}, u32[]{:S(2)}) collective-permute-start(bf16[8,9,16,128]{3,2,1,0:T(8,128)(2,1)S(1)} %all-to-all-done.refs_1_.refs_3_), channel_id=1, source_target_pairs={{0,2},{1,3},{2,0},{3,1},{4,6},{5,7},{6,4},{7,5},{8,10},{9,11},{10,... | collective-permute-start | bytes 884744 | tf_op jit(solution)/shard_map/ppermute | solution.py:249
  44.2 9.6 %collective-permute-start = (bf16[8,9,16,128]{3,2,1,0:T(8,128)(2,1)S(1)}, bf16[8,9,16,128]{3,2,1,0:T(8,128)(2,1)S(1)}, u32[]{:S(2)}, u32[]{:S(2)}) collective-permute-start(bf16[8,9,16,128]{3,2,1,0:T(8,128)(2,1)S(1)} %all-to-all-done.refs_1_.refs_3_), channel_id=1, source_target_pairs={{0,1},{1,0},{2,3},{3,2},{4,5},{5,4},{6,7},{7,6},{8,9},{9,8},{10,11... | collective-permute-start | bytes 884744 | tf_op jit(solution)/shard_map/ppermute | solution.py:249
  51.7 2.1 %collective-permute-start.1 = (bf16[8,9,16,128]{3,2,1,0:T(8,128)(2,1)S(1)}, bf16[8,9,16,128]{3,2,1,0:T(8,128)(2,1)S(1)}, u32[]{:S(2)}, u32[]{:S(2)}) collective-permute-start(bf16[8,9,16,128]{3,2,1,0:T(8,128)(2,1)S(1)} %all-to-all-done.1.refs_2_.refs_4_), channel_id=1, source_target_pairs={{0,1},{1,0},{2,3},{3,2},{4,5},{5,4},{6,7},{7,6},{8,9},{9,8},{10,11... | collective-permute-start | bytes 884744 | tf_op jit(solution)/shard_map/ppermute | solution.py:249
  51.7 2.1 %collective-permute-start.3 = (bf16[8,9,16,128]{3,2,1,0:T(8,128)(2,1)S(1)}, bf16[8,9,16,128]{3,2,1,0:T(8,128)(2,1)S(1)}, u32[]{:S(2)}, u32[]{:S(2)}) collective-permute-start(bf16[8,9,16,128]{3,2,1,0:T(8,128)(2,1)S(1)} %collective-permute-done.2.refs_3_), channel_id=1, source_target_pairs={{0,1},{1,0},{2,3},{3,2},{4,5},{5,4},{6,7},{7,6},{8,9},{9,8},{10,11... | collective-permute-start | bytes 884744 | tf_op jit(solution)/shard_map/ppermute | solution.py:249
  52.2 8.9 %collective-permute-start.4 = (bf16[8,9,16,128]{3,2,1,0:T(8,128)(2,1)S(1)}, bf16[8,9,16,128]{3,2,1,0:T(8,128)(2,1)S(1)}, u32[]{:S(2)}, u32[]{:S(2)}) collective-permute-start(bf16[8,9,16,128]{3,2,1,0:T(8,128)(2,1)S(1)} %all-to-all-done.1.refs_2_.refs_4_), channel_id=1, source_target_pairs={{0,2},{1,3},{2,0},{3,1},{4,6},{5,7},{6,4},{7,5},{8,10},{9,11},{10,... | collective-permute-start | bytes 884744 | tf_op jit(solution)/shard_map/ppermute | solution.py:249
  61.2 1.6 %collective-permute-start.5 = (bf16[8,9,16,128]{3,2,1,0:T(8,128)(2,1)S(1)}, bf16[8,9,16,128]{3,2,1,0:T(8,128)(2,1)S(1)}, u32[]{:S(2)}, u32[]{:S(2)}) collective-permute-start(bf16[8,9,16,128]{3,2,1,0:T(8,128)(2,1)S(1)} %collective-permute-done.4.refs_4_), channel_id=1, source_target_pairs={{0,1},{1,0},{2,3},{3,2},{4,5},{5,4},{6,7},{7,6},{8,9},{9,8},{10,11... | collective-permute-start | bytes 884744 | tf_op jit(solution)/shard_map/ppermute | solution.py:249
